TPU v7x, 128 devices: a whole 4x4x4 slice. The times are simulated.
128 devices in a mesh: seq: 4 (over z), tm: 32 (over y, x, core).
Axes of the slice: x: 4, y: 4, z: 4, core: 2. Of those that a mesh axis runs over, the one named last changes fastest.
Arguments:
- inputs: float32 [4, 8192, 64], P('seq', 'tm'), may hold values from -6 to 6
- guess: float32 [4, 8192, 64], P('seq', 'tm'), may hold values from -0.9 to 0.9
- cotangent: float32 [4, 8192, 64], P('seq', 'tm'), may hold values from -0.4 to 0.4
- w_input: float32 [64, 192], replicated, may hold values from -0.75 to 0.75
- w_hidden: float32 [64, 192], replicated, may hold values from -0.75 to 0.75
- bias: float32 [256], replicated, may hold values from -2 to 13, as said below
Outputs:
- new_states: float32 [4, 8192, 64], P('seq', 'tm')
- adjoint: float32 [4, 8192, 64], P('seq', 'tm')
- grad_input: float32 [64, 192], replicated
- grad_hidden: float32 [64, 192], replicated
- grad_bias: float32 [256], replicated
Inputs may be any that keep to these rules, and one draw needn't show every extreme that they name: `bias`: gate biases as laid out in the meaning.
All inputs are finite; a program needn't handle non-finite values.
Results may differ from a plain program's by a relative error of at most 0.00075.
Values sent between devices are 32-bit elements; how exact they have to be, the bound alone decides.
No kernel may reach another device: no remote copies, remote signals or barrier semaphores. Data moves between devices by JAX's collectives and lax.ppermute only.
A program may use at most 128 MiB of HBM per device.

v0:
```python
import math

import jax
import jax.numpy as jnp
from jax import lax
from jax.sharding import PartitionSpec as P

HIGHEST = lax.Precision.HIGHEST


def shifted(x, axis, by):
    count = lax.axis_size(axis)
    pairs = [(i, i + by) for i in range(count) if 0 <= i + by < count]
    return lax.ppermute(x, axis, pairs)


def prefix(value, axis, join, neutral, backward):
    count, mine = (lax.axis_size(axis), lax.axis_index(axis))
    pieces = jax.tree.map(lambda part: lax.all_gather(part, axis), value)
    if backward:
        pieces = jax.tree.map(lambda part: part[::-1], pieces)
        mine = count - 1 - mine
    total = jax.tree.map(
        lambda part, zero: jnp.full_like(part, 0) + jnp.asarray(zero, part.dtype), value, neutral
    )

    def lap(position, total):
        longer = join(total, jax.tree.map(lambda part: part[position], pieces))
        return jax.tree.map(lambda new, old: jnp.where(position < mine, new, old), longer, total)

    return lax.fori_loop(0, count - 1, lap, total)


def cell(inputs, prev, w_input, w_hidden, bias):
    width = prev.shape[-1]
    gate_in = jnp.einsum("...d,dk->...k", inputs, w_input, precision=HIGHEST) + bias[: 3 * width]
    gate_hid = jnp.einsum("...j,jk->...k", prev, w_hidden, precision=HIGHEST)
    reset = jax.nn.sigmoid(gate_in[..., :width] + gate_hid[..., :width])
    update = jax.nn.sigmoid(gate_in[..., width : 2 * width] + gate_hid[..., width : 2 * width])
    hsum = gate_hid[..., 2 * width :] + bias[3 * width :]
    cand = jnp.tanh(gate_in[..., 2 * width :] + reset * hsum)
    value = (1.0 - update) * cand + update * prev
    return (value, (reset, update, cand, hsum))


def jacobian(prev, w_hidden, reset, update, cand, hsum):
    width = prev.shape[-1]
    w_reset = w_hidden[:, :width].T
    w_update = w_hidden[:, width : 2 * width].T
    w_cand = w_hidden[:, 2 * width :].T
    squash = (1.0 - update) * (1.0 - cand * cand)
    coef_cand = squash * reset
    coef_reset = squash * hsum * reset * (1.0 - reset)
    coef_update = (prev - cand) * update * (1.0 - update)
    identity_mat = jnp.eye(width, dtype=jnp.float32)
    return (
        coef_cand[..., :, None] * w_cand
        + coef_reset[..., :, None] * w_reset
        + coef_update[..., :, None] * w_update
        + update[..., :, None] * identity_mat
    )


def compose(earlier, later):
    matrix = jnp.einsum("...ij,...jk->...ik", later[0], earlier[0], precision=HIGHEST)
    offset = jnp.einsum("...ij,...j->...i", later[0], earlier[1], precision=HIGHEST) + later[1]
    return (matrix, offset)


def block_prefix(mats, offs):
    seqs_here, length, width = offs.shape
    run = 16
    groups = length // run
    mats_run = mats.reshape(seqs_here, groups, run, width, width)
    offs_run = offs.reshape(seqs_here, groups, run, width)
    current = (mats_run[:, :, 0], offs_run[:, :, 0])
    mat_list = [current[0]]
    off_list = [current[1]]
    for position in range(1, run):
        current = compose(current, (mats_run[:, :, position], offs_run[:, :, position]))
        mat_list.append(current[0])
        off_list.append(current[1])
    inner_mat = jnp.stack(mat_list, axis=2)
    inner_off = jnp.stack(off_list, axis=2)
    totals = (jnp.moveaxis(current[0], 1, 0), jnp.moveaxis(current[1], 1, 0))
    unit = (
        jnp.broadcast_to(jnp.eye(width, dtype=jnp.float32), (seqs_here, width, width)),
        jnp.zeros((seqs_here, width), jnp.float32),
    )

    def carry_step(carry, item):
        return (compose(carry, item), carry)

    unused, before = lax.scan(carry_step, unit, totals)
    before_mat = jnp.moveaxis(before[0], 0, 1)[:, :, None]
    before_off = jnp.moveaxis(before[1], 0, 1)[:, :, None]
    full_mat, full_off = compose((before_mat, before_off), (inner_mat, inner_off))
    return (
        full_mat.reshape(seqs_here, length, width, width),
        full_off.reshape(seqs_here, length, width),
    )


def per_device(inputs, guess, cotangent, w_input, w_hidden, bias):
    seqs_here, steps_here, width = guess.shape
    tm_count = lax.axis_size("tm")
    incoming = shifted(guess[:, -1:, :], "tm", 1)
    prev = jnp.concatenate([incoming, guess[:, :-1]], axis=1)
    value, parts = cell(inputs, prev, w_input, w_hidden, bias)
    jac = jacobian(prev, w_hidden, *parts)
    shift = value - jnp.einsum("slij,slj->sli", jac, prev, precision=HIGHEST)
    prefix_mat, prefix_off = block_prefix(jac, shift)
    block_mat = prefix_mat[:, -1]
    block_off = prefix_off[:, -1]
    jac_t = jnp.swapaxes(jac, -1, -2)
    identity_mat = jnp.broadcast_to(jnp.eye(width, dtype=jnp.float32), (seqs_here, 1, width, width))
    steps_mat = jnp.flip(jnp.concatenate([jac_t[:, 1:], identity_mat], axis=1), axis=1)
    steps_off = jnp.flip(cotangent, axis=1)
    suffix_mat, suffix_off = block_prefix(steps_mat, steps_off)
    back_mat = jnp.einsum("sij,sjk->sik", jac_t[:, 0], suffix_mat[:, -1], precision=HIGHEST)
    back_off = jnp.einsum("sij,sj->si", jac_t[:, 0], suffix_off[:, -1], precision=HIGHEST)
    zero_state = jnp.zeros((seqs_here, width), jnp.float32)
    unit = (identity_mat[:, 0], zero_state)
    state_in = prefix((block_mat, block_off), "tm", compose, unit, False)[1]
    adjoint_in = prefix((back_mat, back_off), "tm", compose, unit, True)[1]
    new_states = jnp.einsum("slij,sj->sli", prefix_mat, state_in, precision=HIGHEST) + prefix_off
    adjoint = jnp.flip(
        jnp.einsum("slij,sj->sli", suffix_mat, adjoint_in, precision=HIGHEST) + suffix_off, axis=1
    )
    unused, pullback = jax.vjp(
        lambda a, b, c: cell(inputs, prev, a, b, c)[0], w_input, w_hidden, bias
    )
    local_a, local_b, local_c = pullback(adjoint)
    grad_a, grad_b, grad_c = lax.psum((local_a, local_b, local_c), ("seq", "tm"))
    total_steps = lax.axis_size("seq") * seqs_here * tm_count * steps_here
    scale = 1.0 / math.sqrt(total_steps)
    return (new_states, adjoint, grad_a * scale, grad_b * scale, grad_c * scale)


def solution(mesh):
    return jax.shard_map(
        per_device,
        mesh=mesh,
        in_specs=(P("seq", "tm", None), P("seq", "tm", None), P("seq", "tm", None), P(), P(), P()),
        out_specs=(P("seq", "tm", None), P("seq", "tm", None), P(), P(), P()),
        check_vma=False,
    )
```

profile of v0, /device:TPU:1, one launch (start us, length us, event | category | flops | bytes accessed | tf_op | source)
XLA Modules:
  0.0 539.1 jit_solution(10686293711907900571)
XLA Ops:
  8.1 4.5 collective-permute-start
  21.7 2.1 add_bitcast_fusion
  23.8 3.3 copy-done.7
  28.8 4.3 pad_maximum_fusion
  33.0 8.4 %rev.17 = f32[1,256,64,64]{3,2,1,0:T(8,128)} reverse(f32[1,256,64,64]{3,2,1,0:T(8,128)} %pad_maximum_fusion), dimensions={1} | reverse | bytes 8388608 | tf_op jit(solution)/shard_map/jit(_flip)/rev | solution.py:117
  41.4 2.1 fusion.84
  47.0 2.0 fusion.87
  54.9 2.0 fusion.95
  56.9 2.0 fusion.97
  83.0 3.3 copy-done.6
  86.4 6.5 %while.61 = (s32[]{:T(128)}, f32[1,64,64]{2,1,0:T(8,128)S(1)}, f32[1,64]{1,0:T(1,128)S(1)}, f32[16,1,64,64]{3,2,1,0:T(8,128)S(1)}, f32[16,1,64]{2,1,0:T(1,128)S(...) while((s32[]{:T(128)}, f32[1,64,64]{2,1,0:T(8,128)S(1)}, ...), condition=%wide.region_5.6_spmd, body=%wide.region_4.5_spmd.sunk | while | flops 3194946 | bytes 216929 | solution.py:94
  92.9 22.0 %fusion.40 = f32[16,1,16,64]{3,1,2,0:T(1,128)S(1)} fusion(f32[16,1,64]{2,1,0:T(1,128)S(1)} %get-tuple-element.273, f32[1,16,16,64,64]{4,3,1,2,0:T(8,128)} %copy-done.6), kind=kOutput, calls=%fused_computation.59 | convolution fusion | flops 12582912 | bytes 4263936 | tf_op jit(solution)/shard_map/...ij,...j->...i/dot_general | solution.py:66
  116.2 62.1 %all-reduce.6 = f32[2048]{0:T(1024)S(1)} all-reduce(f32[2048]{0:T(1024)S(1)} %dynamic-update-slice), channel_id=3, replica_groups=mesh['seq'=4,'tm'=32] {'tm'}, use_global_device_ids=true, to_apply=%add.6 | all-reduce | flops 2048 | bytes 16384
  178.4 10.3 %fusion.42 = f32[16,16,64,64]{3,2,1,0:T(8,128)S(1)} fusion(f32[16,1,64,64]{3,2,1,0:T(8,128)S(1)} %get-tuple-element.272, f32[1,16,16,64,64]{4,3,1,2,0:T(8,128)} %copy-done.6), kind=kOutput, calls=%fused_computation.61 | convolution fusion | flops 805306368 | bytes 8650752 | tf_op jit(solution)/shard_map/...ij,...jk->...ik/dot_general | solution.py:65
  188.7 3.3 copy-done.9
  192.9 26.2 %all-gather = f32[2048,64]{1,0:T(8,128)S(1)} all-gather(f32[64,64]{1,0:T(8,128)S(1)} %fusion.139), channel_id=2, replica_groups=mesh['seq'=4,'tm'=32] {'tm'}, dimensions={0}, use_global_device_ids=true | all-gather | bytes 540672 | tf_op jit(solution)/shard_map/all_gather | solution.py:19
  219.3 5.8 %while.63 = (s32[]{:T(128)}, f32[1,64]{1,0:T(1,128)S(1)}, s32[]{:T(128)}, f32[32,1,64,64]{3,2,1,0:T(8,128)S(1)}, f32[32,1,64]{2,1,0:T(1,128)S(1)}, /*index=5*/s32[]{:T(128)}, s32[]{:T(128)}) while((s32[]{:T(128)}, f32[1,64]{1,0:T(1,128)S(1)}, s32[]{:T(128)}, f32[32,1,64,64]{3,2,1,0:T(8,128)S(1)}, f32[32,1,64]{2,1,0:T(1,128)S(1)}, ...), condition=%wide.region_7.8_spmd.clone, body=%wide.region_6.7_spmd.clone.sunk | while | flops 49412 | bytes 37727 | solution.py:31
  225.0 5.6 %multiply_reduce_fusion = f32[256,64]{1,0:T(8,128)S(1)} fusion(f32[64,256,64]{0,2,1:T(8,128)} %bitcast.993, f32[64]{0:T(128)S(1)} %bitcast.1113), kind=kLoop, calls=%fused_computation.55 | loop fusion | flops 2080768 | bytes 4260096
  231.1 2.8 multiply_reduce_fusion.2
  236.0 9.4 %multiply_add_fusion = f32[1,16,16,64,64]{4,3,1,2,0:T(8,128)S(1)} fusion(f32[64,64]{1,0:T(8,128)S(1)} %fusion.140, f32[16,16,64]{2,0,1:T(8,128)S(1)} %copy.333, f32[64,64]{1,0:T(8,128)S(1)} %copy.331, f32[16,16,64]{2,0,1:T(8,128)S(1)} %copy.330, f32[64,64]{1,0:T(8,128)S(1)} %copy.328, f32[16,16,64]{2,0,1:T(8,128)S(1)} %copy.327, f32[64,64]{1,0:T(8,128)S(1)} %copy.325, ...), kind=kLoop, calls=%fused_computation.58 | loop fusion | flops 7340032 | bytes 4521984 | tf_op jit(solution)/shard_map/add | solution.py:57
  250.6 2.1 fusion.58
  252.8 2.4 fusion.60
  288.1 3.3 copy-done.4
  291.5 6.5 %while.60 = (s32[]{:T(128)}, f32[1,64,64]{2,1,0:T(8,128)S(1)}, f32[1,64]{1,0:T(1,128)S(1)}, f32[16,1,64,64]{3,2,1,0:T(8,128)S(1)}, f32[16,1,64]{2,1,0:T(1,128)S(...) while((s32[]{:T(128)}, f32[1,64,64]{2,1,0:T(8,128)S(1)}, ...), condition=%wide.region_1.2_spmd, body=%wide.region_0.1_spmd.sunk | while | flops 3194946 | bytes 216929 | solution.py:94
  298.0 22.0 %fusion.44 = f32[16,1,16,64]{3,1,2,0:T(1,128)S(1)} fusion(f32[16,1,64]{2,1,0:T(1,128)S(1)} %get-tuple-element.270, f32[1,16,16,64,64]{4,3,1,2,0:T(8,128)} %copy-done.4), kind=kOutput, calls=%fused_computation.63 | convolution fusion | flops 12582912 | bytes 4263936 | tf_op jit(solution)/shard_map/...ij,...j->...i/dot_general | solution.py:66
  320.2 21.5 %all_gather.19 = f32[32,1,64]{2,1,0:T(1,128)S(1)} all-gather(f32[1,1,64]{2,1,0:T(1,128)S(1)} %slice.380), channel_id=1, replica_groups=mesh['seq'=4,'tm'=32] {'tm'}, dimensions={0}, use_global_device_ids=true | all-gather | bytes 8448 | tf_op jit(solution)/shard_map/all_gather | solution.py:19
  341.6 8.4 %fusion.46 = f32[16,16,64,64]{3,2,1,0:T(8,128)S(1)} fusion(f32[16,1,64,64]{3,2,1,0:T(8,128)S(1)} %get-tuple-element.269, f32[1,16,16,64,64]{4,3,1,2,0:T(8,128)S(1)} %copy-done.5), kind=kOutput, calls=%fused_computation.65 | convolution fusion | flops 805306368 | bytes 8650752 | tf_op jit(solution)/shard_map/...ij,...jk->...ik/dot_general | solution.py:65
  350.1 3.3 copy-done.8
  353.4 22.2 %all_gather.18 = f32[32,1,64,64]{3,2,1,0:T(8,128)S(1)} all-gather(f32[1,1,64,64]{3,2,1,0:T(8,128)S(1)} %slice.379), channel_id=1, replica_groups=mesh['seq'=4,'tm'=32] {'tm'}, dimensions={0}, use_global_device_ids=true | all-gather | bytes 540672 | tf_op jit(solution)/shard_map/all_gather | solution.py:19
  375.6 5.7 %while.62 = (s32[]{:T(128)}, f32[1,64]{1,0:T(1,128)S(1)}, s32[]{:T(128)}, f32[32,1,64,64]{3,2,1,0:T(8,128)S(1)}, f32[32,1,64]{2,1,0:T(1,128)S(1)}, /*index=5*/s32[]{:T(128)}, s32[]{:T(128)}) while((s32[]{:T(128)}, f32[1,64]{1,0:T(1,128)S(1)}, s32[]{:T(128)}, f32[32,1,64,64]{3,2,1,0:T(8,128)S(1)}, f32[32,1,64]{2,1,0:T(1,128)S(1)}, ...), condition=%wide.region_3.4_spmd.clone, body=%wide.region_2.3_spmd.clone.sunk | while | flops 49412 | bytes 37727 | solution.py:31
  382.0 5.6 %multiply_reduce_fusion.1 = f32[256,64]{1,0:T(8,128)S(1)} fusion(f32[64,256,64]{0,2,1:T(8,128)} %bitcast.991, f32[64]{0:T(128)S(1)} %bitcast.1112), kind=kLoop, calls=%fused_computation.56 | loop fusion | flops 2080768 | bytes 4260096 | tf_op jit(solution)/shard_map/slij,sj->sli/dot_general | solution.py:126
  388.4 140.9 %all-reduce.10.cloned.1.call-done = (f32[64,192]{1,0:T(8,128)}, f32[64,192]{1,0:T(8,128)}, f32[256]{0:T(256)}) async-done(((f32[64,192]{1,0:T(8,128)}, f32[64,192]{1,0:T(8,128)}, f32[256]{0:T(256)}), (f32[64,192]{1,0:T(8,128)}, f32[64,192]{1,0:T(8,128)}, f32[256]{0:T(256)})) %all-reduce.10.cloned.1.call-update) | async-done | bytes 99344 | tf_op jit(solution)/shard_map/psum | solution.py:134
  (500 shorter events, 114.4 us)
Async XLA Ops:
  7.2 9.5 %copy-start = (f32[1,256,64]{1,2,0:T(8,128)S(1)}, f32[1,256,64]{1,2,0:T(8,128)}, u32[]{:S(2)}) copy-start(f32[1,256,64]{1,2,0:T(8,128)} %param.14) | copy-start | bytes 196612
  7.2 522.1 %all-reduce.10.cloned.1.call-start = ((), (), s32[]{:S(2)}) async-start(), calls=%async_computation | async-start | bytes 264192 | tf_op jit(solution)/shard_map/psum | solution.py:134
  8.1 11.7 %collective-permute-start = (f32[1,1,64]{1,2,0:T(8,128)S(1)}, f32[1,1,64]{1,2,0:T(8,128)S(1)}, u32[]{:S(2)}, u32[]{:S(2)}) collective-permute-start(f32[1,1,64]{1,2,0:T(8,128)S(1)} %slice.260), channel_id=1, source_target_pairs={{0,1},{1,2},{2,3},{3,4},{4,5},{5,6},{6,7},{7,8},{8,9},{9,10},{10,1... | collective-permute-start | bytes 776 | tf_op jit(solution)/shard_map/ppermute | solution.py:14
  13.5 15.3 %copy-start.10 = (f32[1,64,64]{2,1,0:T(8,128)}, f32[1,64,64]{2,1,0:T(8,128)S(1)}, u32[]{:S(2)}) copy-start(f32[1,64,64]{2,1,0:T(8,128)S(1)} %fusion.141) | copy-start | bytes 49156
  23.8 3.3 copy-start.7
  41.4 31.4 %copy-start.3 = (f32[1,256,64,64]{3,2,1,0:T(8,128)S(1)}, f32[1,256,64,64]{3,2,1,0:T(8,128)}, u32[]{:S(2)}) copy-start(f32[1,256,64,64]{3,2,1,0:T(8,128)} %rev.17) | copy-start | bytes 12582916
  77.8 8.6 %copy-start.12 = (f32[1,64,64]{2,1,0:T(8,128)S(1)}, f32[1,64,64]{2,1,0:T(8,128)}, u32[]{:S(2)}) copy-start(f32[1,64,64]{2,1,0:T(8,128)} %copy-done.10) | copy-start | bytes 49156
  83.0 3.3 copy-start.6
  188.7 3.3 copy-start.9
  231.1 24.1 %copy-start.13 = (f32[256,64]{0,1:T(8,128)}, f32[256,64]{0,1:T(8,128)S(1)}, u32[]{:S(2)}) copy-start(f32[256,64]{0,1:T(8,128)S(1)} %reverse.3) | copy-start | bytes 196612
  245.3 3.3 copy-start.1
  250.6 28.2 %copy-start.2 = (f32[1,16,16,64,64]{4,3,1,2,0:T(8,128)S(1)}, f32[1,16,16,64,64]{4,3,1,2,0:T(8,128)}, u32[]{:S(2)}) copy-start(f32[1,16,16,64,64]{4,3,1,2,0:T(8,128)} %copy-done.1) | copy-start | bytes 12582916
  282.9 8.6 %copy-start.11 = (f32[1,64,64]{2,1,0:T(8,128)S(1)}, f32[1,64,64]{2,1,0:T(8,128)}, u32[]{:S(2)}) copy-start(f32[1,64,64]{2,1,0:T(8,128)} %copy-done.10) | copy-start | bytes 49156
  288.1 3.3 copy-start.4
  298.0 43.6 %copy-start.5 = (f32[1,16,16,64,64]{4,3,1,2,0:T(8,128)S(1)}, f32[1,16,16,64,64]{4,3,1,2,0:T(8,128)}, u32[]{:S(2)}) copy-start(f32[1,16,16,64,64]{4,3,1,2,0:T(8,128)} %copy-done.4) | copy-start | bytes 12582916
  350.0 3.3 copy-start.8
Sparse Core Ops, SparseCore 0:
  387.7 141.4 all-reduce.9
where the time goes:
time: 544 us; the launch traced here: 539 us
  matrix products  171 us (31%)
  waiting for transfers between devices  141 us (26%)
  blocking collectives  132 us (24%)
  local copies, waits for them, and re-layouts  39.5 us (7%)
  other arithmetic  34.2 us (6%)
  between operations  15.8 us (3%)
    psum x1, waiting for transfers between devices, per_device(): lax.psum((local_a, local_b, local_c), ('seq', 'tm'))  141 us
    dot_general x126, matrix products, compose(): jnp.einsum('...ij,...j->...i', later[0], earlier[1], precision=HIGHEST)  119 us
    all_gather x3, blocking collectives, prefix(): pieces = jax.tree.map(lambda part: lax.all_gather(part, axis), value)  69.9 us
    unnamed x1, blocking collectives  62.1 us
    dot_general x64, matrix products, compose(): jnp.einsum('...ij,...jk->...ik', later[0], earlier[0], precision=HIGHEST)  45 us
    unnamed x37, local copies, waits for them, and re-layouts  22 us
  transfers between devices with their start and end apart: 2, of which 1 were waited for; matrix products, arithmetic and copies ran while one was open for 1% of the time, Pallas kernels for 0%

commit v1 on v0

v1 whole, which is shorter than its diff:
```python
import math

import jax
import jax.numpy as jnp
from jax import lax
from jax.experimental import pallas as pl
from jax.experimental.pallas import tpu as pltpu
from jax.sharding import PartitionSpec as P

F32 = jnp.float32
BF16 = jnp.bfloat16
HIGHEST = lax.Precision.HIGHEST
H = 64
T = 256
RUN = 16
PAIRS = 8
DEV = 32
HALF = DEV // 2
TILE = 40
VMEM_LIMIT = 48 * 1024 * 1024


def dot(a, b, dims=((1,), (0,))):
    return lax.dot_general(a, b, (dims, ((), ())), precision=HIGHEST, preferred_element_type=F32)


def bdot(a, b):
    return jnp.dot(a, b, preferred_element_type=F32)


def iota(shape, axis):
    return lax.broadcasted_iota(jnp.int32, shape, axis)


def split(a):
    high = a.astype(BF16)
    return high, (a - high.astype(F32)).astype(BF16)


def sigmoid(a):
    return 1.0 / (1.0 + jnp.exp(-a))


def doubled(block):
    zero = jnp.zeros_like(block)
    return jnp.concatenate(
        [jnp.concatenate([block, zero], axis=1), jnp.concatenate([zero, block], axis=1)], axis=0
    )


def forward_weights(wh):
    wide = jnp.concatenate(
        [doubled(wh[:, 128:192]), doubled(wh[:, :64]), doubled(wh[:, 64:128])], axis=1
    )
    high, low = split(wide)
    return jnp.concatenate([high, high, low], axis=0)


def backward_weights(wh):
    tall = jnp.concatenate(
        [doubled(wh[:, 128:192].T), doubled(wh[:, :64].T), doubled(wh[:, 64:128].T)], axis=0
    )
    high, low = split(tall)
    return jnp.concatenate([high, high, low], axis=0)


def three(a):
    high, low = split(a)
    return jnp.concatenate([high, low, high], axis=1)


def to_row(column, offset):
    hit = iota((H, 128), 1) == iota((H, 128), 0) + offset
    return jnp.sum(jnp.where(hit, column, 0.0), axis=0, keepdims=True)


def gate_terms(gi_r, gi_z, gi_n, gh_r, gh_z, gh_n, bias_h, prev):
    reset = sigmoid(gi_r + gh_r)
    update = sigmoid(gi_z + gh_z)
    keep = sigmoid(-(gi_z + gh_z))
    hsum = gh_n + bias_h
    cand = jnp.tanh(gi_n + reset * hsum)
    squash = keep * (1.0 - cand * cand)
    p = squash * reset
    q = squash * hsum * reset * (1.0 - reset)
    w = (prev - cand) * update * keep
    shift = keep * cand - p * gh_n - q * gh_r - w * gh_z
    return squash, p, q, w, update, shift


def packed(a):
    return jnp.concatenate([a[:, :128], a[:, 128:]], axis=0).T


def combine(earlier, later):
    row, lane = iota((72, 128), 0), iota((72, 128), 1)
    product = dot(earlier[:, :H], later[:H, :])
    return (
        product
        + jnp.where((lane == H) & (row < H), earlier, 0.0)
        + jnp.where((row == H) & (lane < H), later, 0.0)
    )


def blocks_kernel(
    x_ref, g_ref, c_ref, wi_ref, wh_ref, bias_ref,
    send_ref, aug_ref, sup_ref, pk_ref, tl_ref,
    y_ref, z_ref, b_ref, lhs_ref, w_ref,
):
    wh = wh_ref[...]
    w_ref[...] = forward_weights(wh)
    guess = g_ref[...]
    prev = pltpu.roll(guess, 1, 1)
    gi = dot(wi_ref[...], x_ref[...], ((0,), (0,)))
    gh = dot(wh, prev, ((0,), (0,)))
    bias0 = jnp.broadcast_to(bias_ref[0:1, :], (128, 128)).T
    bias1 = jnp.broadcast_to(bias_ref[1:2, :], (128, 128)).T
    bias0 = jnp.concatenate([bias0, bias0], axis=1)
    bias1 = jnp.concatenate([bias1, bias1], axis=1)
    gi_r = gi[:64] + bias0[:64]
    gi_z = gi[64:128] + bias0[64:]
    gi_n = gi[128:] + bias1[:64]
    squash, p, q, w, u, shift = gate_terms(
        gi_r, gi_z, gi_n, gh[:64], gh[64:128], gh[128:], bias1[64:], prev
    )
    tl_ref[0], tl_ref[1], tl_ref[2], tl_ref[3] = squash, p, q, w
    first = iota((H, T), 1) == 0
    pk_ref[0] = packed(jnp.where(first, 0.0, p))
    pk_ref[1] = packed(jnp.where(first, 0.0, q))
    pk_ref[2] = packed(jnp.where(first, 0.0, w))
    pk_ref[3] = packed(jnp.where(first, 1.0, u))
    pk_ref[4] = packed(jnp.where(first, 0.0, shift))
    pk_ref[5] = packed(c_ref[...])

    lane64 = iota((H, 128), 1)
    low64 = lane64 < H
    eye2 = jnp.where((lane64 == iota((H, 128), 0)) | (lane64 == iota((H, 128), 0) + H), 1.0, 0.0)
    wn2 = jnp.concatenate([wh[:, 128:192], wh[:, 128:192]], axis=1)
    wr2 = jnp.concatenate([wh[:, :64], wh[:, :64]], axis=1)
    wz2 = jnp.concatenate([wh[:, 64:128], wh[:, 64:128]], axis=1)

    def rows(k, step):
        return pk_ref[k, pl.ds(step, PAIRS, stride=RUN), :]

    def put(c, value, cot):
        y_ref[c] = value
        high, low = split(value)
        lhs_ref[c * H:(c + 1) * H, 0:128] = high
        lhs_ref[c * H:(c + 1) * H, 128:256] = low
        lhs_ref[c * H:(c + 1) * H, 256:384] = high
        return value * cot

    def put_b(value):
        b_ref[...] = value
        lhs_ref[512:528, :] = three(jnp.concatenate([value, jnp.zeros_like(value)], axis=0))

    p0, q0, w0, u0, s0, c0 = [rows(k, 0) for k in range(6)]
    for c in range(PAIRS):
        value = (
            p0[c:c + 1] * wn2 + q0[c:c + 1] * wr2 + w0[c:c + 1] * wz2 + u0[c:c + 1] * eye2
        )
        z_ref[c] = put(c, value, c0[c:c + 1])
    put_b(s0)

    def step(l, carry):
        p1, q1, w1, u1, s1, c1 = [rows(k, l) for k in range(6)]
        prod = bdot(lhs_ref[...], w_ref[...])
        for c in range(PAIRS):
            part = prod[c * H:(c + 1) * H]
            value = (
                u1[c:c + 1] * y_ref[c] + p1[c:c + 1] * part[:, :128]
                + q1[c:c + 1] * part[:, 128:256] + w1[c:c + 1] * part[:, 256:]
            )
            z_ref[c] += put(c, value, c1[c:c + 1])
        part = prod[512:520]
        put_b(u1 * b_ref[...] + p1 * part[:, :128] + q1 * part[:, 128:256] + w1 * part[:, 256:] + s1)
        return carry

    lax.fori_loop(1, RUN, step, 0)

    low8 = iota((8, 128), 1) < H
    top8 = iota((8, 128), 0) == 0
    bs = b_ref[...]
    for c in range(PAIRS):
        y = y_ref[c]
        z = z_ref[c]
        offs = jnp.broadcast_to(bs[c:c + 1], (8, 128))
        for part in range(2):
            if part:
                y, z, offs = pltpu.roll(y, H, 1), pltpu.roll(z, H, 1), pltpu.roll(offs, H, 1)
            col = jnp.sum(jnp.where(low64, z, 0.0), axis=1, keepdims=True)
            n = c + part * PAIRS
            aug_ref[n, 0:64, :] = jnp.where(low64, y, jnp.where(lane64 == H, col, 0.0))
            aug_ref[n, 64:72, :] = jnp.where(low8 & top8, offs, 0.0)
    sups = []
    for k in range(4):
        left = combine(aug_ref[4 * k], aug_ref[4 * k + 1])
        right = combine(aug_ref[4 * k + 2], aug_ref[4 * k + 3])
        sups.append(combine(left, right))
        sup_ref[k] = sups[-1]
    total = combine(combine(sups[0], sups[1]), combine(sups[2], sups[3]))

    low32 = iota((32, 128), 1) < H
    body = jnp.where(low32, total[:32], pltpu.roll(total[32:64], H, 1))
    col = jnp.sum(jnp.where(lane64 == H, total[:64], 0.0), axis=1, keepdims=True)
    row_bc = jnp.where(low8[:1], total[64:65], 0.0) + to_row(col, H)
    last = jnp.sum(jnp.where(lane64 == 127, guess[:, 128:], 0.0), axis=1, keepdims=True)

    def head(a):
        return jnp.sum(jnp.where(lane64 == 0, a[:, :128], 0.0), axis=1, keepdims=True)

    row_gr = to_row(last, 0) + to_row(head(gi_r), H)
    row_zn = to_row(head(gi_z), 0) + to_row(head(gi_n), H)
    row8 = iota((8, 128), 0)
    tail = jnp.where(row8 == 0, row_bc, jnp.where(row8 == 1, row_gr, jnp.where(row8 == 2, row_zn, 0.0)))
    for k in range(DEV):
        send_ref[k, 0:32, :] = body
        send_ref[k, 32:40, :] = tail


def apply_kernel(
    me_ref, r_ref, aug_ref, sup_ref, pk_ref, tl_ref, x_ref, g_ref, wh_ref, bias_ref,
    state_ref, adj_ref, grad_ref,
    w_ref, wt_ref, lhs_ref, z_ref, d_ref, row_ref, bnd_ref, st_ref, lam_ref,
):
    me = me_ref[0]
    wh = wh_ref[...]
    w_ref[...] = forward_weights(wh)
    wt_ref[...] = backward_weights(wh)
    bias_h = bias_ref[1:2, 64:]

    bc = r_ref[:, 32, :]
    gr = r_ref[:, 33, :]
    zn = r_ref[:, 34, :]
    prev = jnp.where(iota((DEV, H), 0) == DEV - 1, 0.0, gr[:, :H])
    gr_next = pltpu.roll(gr, DEV - 1, 0)
    zn_next = pltpu.roll(zn, DEV - 1, 0)
    gh = dot(prev, wh)
    terms = gate_terms(
        gr_next[:, H:], zn_next[:, :H], zn_next[:, H:],
        gh[:, :64], gh[:, 64:128], gh[:, 128:], bias_h, prev,
    )
    for k in range(6):
        bnd_ref[k] = jnp.concatenate([terms[k], terms[k]], axis=1)
    bnd_ref[6] = jnp.concatenate([prev, prev], axis=1)
    row_ref[...] = bc

    def pair(a):
        return jnp.concatenate([a[:HALF], a[HALF:]], axis=1)

    p, q, w, u, shift = [pair(terms[k]) for k in (1, 2, 3, 4, 5)]
    lane64 = iota((H, 128), 1)
    row64 = iota((H, 128), 0)
    low32 = iota((32, 128), 1) < H
    for k in range(HALF):
        a, b = r_ref[k, 0:32, :], r_ref[k + HALF, 0:32, :]
        top = jnp.where(low32, a, pltpu.roll(b, H, 1))
        bottom = jnp.where(low32, pltpu.roll(a, H, 1), b)
        value = jnp.concatenate([top, bottom], axis=0)
        z_ref[k] = value
        lhs_ref[k * H:(k + 1) * H, :] = three(value)
    offs = pair(bc[:, :H])
    lhs_ref[HALF * H:, :] = three(offs)
    prod = bdot(lhs_ref[...], w_ref[...])
    for k in range(HALF):
        part = prod[k * H:(k + 1) * H]
        z_ref[k] = (
            u[k:k + 1] * z_ref[k] + p[k:k + 1] * part[:, :128]
            + q[k:k + 1] * part[:, 128:256] + w[k:k + 1] * part[:, 256:]
        )
    part = prod[HALF * H:]
    d_ref[...] = u * offs + p * part[:, :128] + q * part[:, 128:256] + w * part[:, 256:] + shift

    lane1 = iota((1, 128), 1)
    eye_a = lane64 == row64
    eye_b = lane64 == row64 + H

    def fwd(eye, base):
        def lap(k, x):
            col = jnp.sum(jnp.where(eye, x, 0.0), axis=1, keepdims=True)
            return jnp.sum(col * z_ref[k - base], axis=0, keepdims=True) + d_ref[pl.ds(k - base, 1), :]
        return lap

    x = bnd_ref[5, DEV - 1:DEV, :]
    x = lax.fori_loop(0, jnp.minimum(me, HALF), fwd(eye_a, 0), x)
    x = lax.fori_loop(HALF, me, fwd(eye_b, HALF), pltpu.roll(x, H, 1))
    x = pltpu.roll(x, H, 1)

    def bwd(eye, base, turn, keep):
        def lap(i, lam):
            k = base - i
            col = jnp.sum(z_ref[k % HALF] * lam, axis=1, keepdims=True)
            extra = row_ref[pl.ds(k, 1), :]
            if turn:
                extra = pltpu.roll(extra, H, 1)
            return jnp.sum(jnp.where(eye, col, 0.0), axis=0, keepdims=True) + jnp.where(keep, extra, 0.0)
        return lap

    lam = jnp.where(lane1 >= H, row_ref[DEV - 1:DEV, :], 0.0)
    lam = lax.fori_loop(
        0, DEV - 1 - jnp.maximum(me + 1, HALF), bwd(eye_b, DEV - 2, False, lane1 >= H), lam
    )
    lam = lax.fori_loop(
        0, jnp.maximum(HALF - 1 - me, 0), bwd(eye_a, HALF - 1, True, lane1 < H), pltpu.roll(lam, H, 1)
    )
    row_terms = [bnd_ref[k, pl.ds(me, 1), :] for k in range(6)]
    lam8 = jnp.broadcast_to(lam, (8, 128))[:, :H]
    wide = jnp.concatenate([lam8 * row_terms[k][:, :H] for k in (1, 2, 3)], axis=1)
    tall = jnp.concatenate([wh[:, 128:192].T, wh[:, :64].T, wh[:, 64:128].T], axis=0)
    carry = (dot(wide, tall) + lam8 * row_terms[4][:, :H])[0:1]
    carry = jnp.where(me == DEV - 1, 0.0, carry)
    carry = jnp.concatenate([carry, jnp.zeros_like(carry)], axis=1)

    row72 = iota((72, 128), 0)
    eye72 = iota((72, 128), 1) == row72
    one = lane1 == H

    def ahead(maps, x):
        col = jnp.sum(jnp.where(eye72, x, 0.0), axis=1, keepdims=True)
        return jnp.where(one, 1.0, jnp.sum(col * maps, axis=0, keepdims=True))

    def back(maps, lam):
        col = jnp.sum(maps[:H] * lam, axis=1, keepdims=True)
        return jnp.where(one, 1.0, jnp.sum(jnp.where(eye_a, col, 0.0), axis=0, keepdims=True))

    starts = [jnp.where(one, 1.0, x)]
    for k in range(3):
        starts.append(ahead(sup_ref[k], starts[-1]))
    ends = [jnp.where(one, 1.0, carry)]
    for k in (3, 2, 1):
        ends.append(back(sup_ref[k], ends[-1]))
    ends = ends[::-1]
    state_rows, carry_rows = [None] * 16, [None] * 16
    for k in range(4):
        value, lam = starts[k], ends[k]
        for j in range(4):
            state_rows[4 * k + j] = value
            carry_rows[4 * k + 3 - j] = lam
            if j < 3:
                value = ahead(aug_ref[4 * k + j], value)
                lam = back(aug_ref[4 * k + 3 - j], lam)

    def gather(items):
        left = jnp.concatenate(items[:8], axis=0)
        right = jnp.concatenate(items[8:], axis=0)
        return jnp.where(iota((8, 128), 1) < H, left, pltpu.roll(right, H, 1))

    def rows(k, step):
        return pk_ref[k, pl.ds(step, PAIRS, stride=RUN), :]

    def pad(a):
        return jnp.concatenate([a, jnp.zeros_like(a)], axis=0)

    def lap(i, both):
        state, kappa = both
        j = RUN - 1 - i
        prod = bdot(three(pad(state)), w_ref[...])[:8]
        lam = rows(5, j) + kappa
        lam_ref[pl.ds(j, PAIRS, stride=RUN), :] = lam
        mixed = jnp.concatenate([lam * rows(0, j), lam * rows(1, j), lam * rows(2, j)], axis=1)
        kappa = bdot(three(pad(mixed)), wt_ref[...])[:8] + lam * rows(3, j)
        state = (
            rows(3, i) * state + rows(0, i) * prod[:, :128] + rows(1, i) * prod[:, 128:256]
            + rows(2, i) * prod[:, 256:] + rows(4, i)
        )
        st_ref[pl.ds(i, PAIRS, stride=RUN), :] = state
        return state, kappa

    lax.fori_loop(0, RUN, lap, (gather(state_rows), gather(carry_rows)))
    states = st_ref[...].T
    state_ref[:, :128] = states[:H]
    state_ref[:, 128:] = states[H:]
    lams = lam_ref[...].T
    lams = jnp.concatenate([lams[:H], lams[H:]], axis=1)
    adj_ref[...] = lams

    before = (me + DEV - 1) % DEV
    first = iota((H, T), 1) == 0

    def with_first(a, k):
        col = jnp.sum(jnp.where(eye_a, bnd_ref[k, pl.ds(before, 1), :], 0.0), axis=1, keepdims=True)
        return jnp.where(first, col, a)

    squash, p, q, w = [with_first(tl_ref[k], k) for k in range(4)]
    prev = with_first(pltpu.roll(g_ref[...], 1, 1), 6)
    left = jnp.concatenate([x_ref[...], prev, jnp.ones((8, T), F32)], axis=0)
    right = jnp.concatenate([lams * q, lams * w, lams * squash, lams * p], axis=0)
    sums = dot(left, right, ((1,), (1,)))
    grad_ref[0:64, :] = sums[:64, :128]
    grad_ref[64:128, :] = sums[64:128, :128]
    grad_ref[128:192, :] = jnp.where(lane64 < H, sums[:64, 128:], sums[64:128, 128:])
    row8 = iota((8, 128), 0)
    grad_ref[192:200, :] = jnp.where(
        row8 == 0, sums[128:136, :128], jnp.where(row8 == 1, sums[128:136, 128:], 0.0)
    )
    grad_ref[200:, :] = jnp.zeros((56, 128), F32)


def shape(*dims):
    return jax.ShapeDtypeStruct(dims, F32)


def per_device(inputs, guess, cotangent, w_input, w_hidden, bias):
    x = jnp.swapaxes(inputs[0], 0, 1)
    g = jnp.swapaxes(guess[0], 0, 1)
    c = jnp.swapaxes(cotangent[0], 0, 1)
    bias2 = bias.reshape(2, 128)
    vmem = pl.BlockSpec(memory_space=pltpu.VMEM)
    params = pltpu.CompilerParams(vmem_limit_bytes=VMEM_LIMIT)
    send, aug, sup, pk, tl = pl.pallas_call(
        blocks_kernel,
        out_shape=(
            shape(DEV, TILE, 128), shape(16, 72, 128), shape(4, 72, 128),
            shape(6, 128, 128), shape(4, H, T),
        ),
        in_specs=[vmem] * 6,
        out_specs=[vmem] * 5,
        scratch_shapes=[
            pltpu.VMEM((PAIRS, H, 128), F32),
            pltpu.VMEM((PAIRS, H, 128), F32),
            pltpu.VMEM((8, 128), F32),
            pltpu.VMEM((528, 384), BF16),
            pltpu.VMEM((384, 384), BF16),
        ],
        compiler_params=params,
        name="blocks",
    )(x, g, c, w_input, w_hidden, bias2)
    received = lax.all_to_all(send, "tm", 0, 0)
    me = lax.axis_index("tm").astype(jnp.int32).reshape(1)
    states, adjoint, grads = pl.pallas_call(
        apply_kernel,
        out_shape=(shape(H, T), shape(H, T), shape(256, 128)),
        in_specs=[pl.BlockSpec(memory_space=pltpu.SMEM)] + [vmem] * 9,
        out_specs=[vmem] * 3,
        scratch_shapes=[
            pltpu.VMEM((384, 384), BF16),
            pltpu.VMEM((1152, 128), BF16),
            pltpu.VMEM((HALF * H + 16, 384), BF16),
            pltpu.VMEM((HALF, H, 128), F32),
            pltpu.VMEM((HALF, 128), F32),
            pltpu.VMEM((DEV, 128), F32),
            pltpu.VMEM((7, DEV, 128), F32),
            pltpu.VMEM((128, 128), F32),
            pltpu.VMEM((128, 128), F32),
        ],
        compiler_params=params,
        name="apply",
    )(me, received, aug, sup, pk, tl, x, g, w_hidden, bias2)
    axes = ("seq", "tm")
    count = lax.axis_size("seq") * lax.axis_size("tm")
    pieces = lax.all_to_all(grads.reshape(count, 2, 128), axes, 0, 0)
    scale = 1.0 / math.sqrt(lax.axis_size("seq") * lax.axis_size("tm") * T)
    mine = jnp.sum(pieces, axis=0) * scale
    whole = lax.all_to_all(jnp.broadcast_to(mine[None], (count, 2, 128)), axes, 0, 0)
    whole = whole.reshape(256, 128)
    grad_input = jnp.concatenate([whole[0:64], whole[128:192, :64]], axis=1)
    grad_hidden = jnp.concatenate([whole[64:128], whole[128:192, 64:]], axis=1)
    grad_bias = whole[192:194].reshape(256)
    return (
        jnp.swapaxes(states, 0, 1)[None], jnp.swapaxes(adjoint, 0, 1)[None],
        grad_input, grad_hidden, grad_bias,
    )


def solution(mesh):
    return jax.shard_map(
        per_device,
        mesh=mesh,
        in_specs=(P("seq", "tm", None), P("seq", "tm", None), P("seq", "tm", None), P(), P(), P()),
        out_specs=(P("seq", "tm", None), P("seq", "tm", None), P(), P(), P()),
        check_vma=False,
    )
```

time: 544 us -> 80 us (0.15)
  matrix products: 171 us -> 0 us
  waiting for transfers between devices: 141 us -> 12.9 us
  blocking collectives: 132 us -> 30.9 us
  local copies, waits for them, and re-layouts: 39.5 us -> 5.56 us
  other arithmetic: 34.2 us -> 0.81 us
  Pallas kernels: 0 us -> 19.9 us
  between operations: 15.8 us -> 0.68 us
    dot_general x196 -> x0, matrix products: 171 us -> none  [the longest x126 119 us: compose(): jnp.einsum('...ij,...j->...i', later[0], earlier[1], precision=HIGHEST)]
    psum x1 -> x0, waiting for transfers between devices: 141 us -> none  [per_device(): lax.psum((local_a, local_b, local_c), ('seq', 'tm'))]
    all_gather x3 -> x0, blocking collectives: 69.9 us -> none  [prefix(): pieces = jax.tree.map(lambda part: lax.all_gather(part, axis), value)]
    unnamed x1 -> x0, blocking collectives: 62.1 us -> none
    all_to_all x0 -> x2, blocking collectives: none -> 30.9 us  [the longest x1 16.7 us: per_device(): pieces = lax.all_to_all(grads.reshape(count, 2, 128), axes, 0, 0)]
    pallas_call x0 -> x2, Pallas kernels: none -> 19.9 us  [the longest x1 10.6 us: per_device(): pl.pallas_call(blocks_kernel, out_shape=(shape(DEV, TILE, 128), shape(16,...]
    unnamed x37 -> x18, local copies, waits for them, and re-layouts: 22 us -> 4.88 us
    all_to_all x0 -> x1, waiting for transfers between devices: none -> 12.9 us  [per_device(): received = lax.all_to_all(send, 'tm', 0, 0)]
  transfers between devices with their start and end apart: 2 -> 1, of which waited for: 1 -> 1; matrix products, arithmetic and copies ran while one was open for 1% -> 0% of each run, Pallas kernels for 0% -> 0%
where the time goes in v1:
time: 80 us; the launch traced here: 79.5 us
  blocking collectives  30.9 us (39%)
  Pallas kernels  19.9 us (25%)
  waiting for transfers between devices  12.9 us (16%)
  starting transfers between devices  8.72 us (11%)
  local copies, waits for them, and re-layouts  5.56 us (7%)
  other arithmetic  0.81 us (1%)
    all_to_all x1, blocking collectives, per_device(): pieces = lax.all_to_all(grads.reshape(count, 2, 128), axes, 0, 0)  16.7 us
    all_to_all x1, blocking collectives, per_device(): lax.all_to_all(jnp.broadcast_to(mine[None], (count, 2, 128)), axes, 0, 0)  14.3 us
    all_to_all x1, waiting for transfers between devices, per_device(): received = lax.all_to_all(send, 'tm', 0, 0)  12.9 us
    pallas_call x1, Pallas kernels, per_device(): pl.pallas_call(blocks_kernel, out_shape=(shape(DEV, TILE, 128), shape(16,...  10.6 us
    pallas_call x1, Pallas kernels, per_device(): pl.pallas_call(apply_kernel, out_shape=(shape(H, T), shape(H, T), shape(2...  9.26 us
    all_to_all x1, starting transfers between devices, per_device(): received = lax.all_to_all(send, 'tm', 0, 0)  8.72 us
    unnamed x18, local copies, waits for them, and re-layouts  4.88 us
  transfers between devices with their start and end apart: 1, of which 1 were waited for; matrix products, arithmetic and copies ran while one was open for 0% of the time, Pallas kernels for 0%

profile of v1, /device:TPU:1, one launch (start us, length us, event | category | flops | bytes accessed | tf_op | source)
XLA Modules:
  0.0 79.5 jit_solution(5653442773976049366)
XLA Ops:
  0.6 0.0 copy-start.8
  0.6 0.7 copy-done.8
  1.3 0.0 copy-start
  1.3 0.8 %copy-done = f32[1,256,64]{1,2,0:T(8,128)S(1)} copy-done((f32[1,256,64]{1,2,0:T(8,128)S(1)}, f32[1,256,64]{1,2,0:T(8,128)}, u32[]{:S(2)}) %copy-start) | copy-done | bytes 65560
  2.2 0.0 copy-start.2
  2.2 0.8 %copy-done.2 = f32[1,256,64]{1,2,0:T(8,128)S(1)} copy-done((f32[1,256,64]{1,2,0:T(8,128)S(1)}, f32[1,256,64]{1,2,0:T(8,128)}, u32[]{:S(2)}) %copy-start.2) | copy-done | bytes 65560
  3.0 0.0 copy-start.4
  3.0 0.8 %copy-done.4 = f32[64,192]{1,0:T(8,128)S(1)} copy-done((f32[64,192]{1,0:T(8,128)S(1)}, f32[64,192]{1,0:T(8,128)}, u32[]{:S(2)}) %copy-start.4) | copy-done | bytes 49176
  3.8 0.0 copy-start.6
  3.8 0.8 %copy-done.6 = f32[1,256,64]{1,2,0:T(8,128)S(1)} copy-done((f32[1,256,64]{1,2,0:T(8,128)S(1)}, f32[1,256,64]{1,2,0:T(8,128)}, u32[]{:S(2)}) %copy-start.6) | copy-done | bytes 65560
  4.7 0.0 copy-start.7
  4.7 0.8 %copy-done.7 = f32[64,192]{1,0:T(8,128)S(1)} copy-done((f32[64,192]{1,0:T(8,128)S(1)}, f32[64,192]{1,0:T(8,128)}, u32[]{:S(2)}) %copy-start.7) | copy-done | bytes 49176
  5.5 10.6 %blocks.1 = (f32[32,40,128]{2,1,0:T(8,128)}, f32[16,72,128]{2,1,0:T(8,128)S(1)}, f32[4,72,128]{2,1,0:T(8,128)S(1)}, f32[6,128,128]{2,1,0:T(8,128)S(1)}, f32[4,64,256]{2,1,0:T(8,128)S(1)}) custom-call(f32[64,256]{1,0:T(8,128)S(1)} %bitcast.23, f32[64,256]{1,0:T(8,128)S(1)} %bitcast.25, f32[64,256]{1,0:T(8,128)S(1)} %bitcast.28, f32[64,192]{1,0:T(8,128)S(1)} %copy-done.7, ...), custom_call_target="tpu_custom_call" | custom-call | tf_op jit(solution)/shard_map/blocks/pallas_call | solution.py:410
  16.2 0.0 copy-start.1
  16.2 0.0 copy-start.3
  16.2 0.0 copy-start.5
  16.2 8.7 %all-to-all-start = ((f32[32,40,128]{2,1,0:T(8,128)}), f32[32,40,128]{2,1,0:T(8,128)S(1)}, u32[]{:S(2)}, u32[]{:S(2)}) async-start(f32[32,40,128]{2,1,0:T(8,128)} %get-tuple-element.13), calls=%async_computation | async-start | bytes 1310720 | tf_op jit(solution)/shard_map/all_to_all | solution.py:428
  24.9 12.9 %all-to-all-done.r_ref = f32[32,40,128]{2,1,0:T(8,128)S(1)} async-done(((f32[32,40,128]{2,1,0:T(8,128)}), f32[32,40,128]{2,1,0:T(8,128)S(1)}, u32[]{:S(2)}, u32[]{:S(2)}) %all-to-all-start) | async-done | bytes 655392 | tf_op jit(solution)/shard_map/all_to_all | solution.py:428
  37.8 0.0 copy-done.1
  37.8 0.0 copy-done.3
  37.8 0.0 copy-done.5
  37.8 9.3 %apply.1 = (f32[64,256]{1,0:T(8,128)}, f32[64,256]{1,0:T(8,128)}, f32[256,128]{1,0:T(8,128)S(1)}) custom-call(s32[1]{0:T(128)} %bitcast.me_ref, f32[32,40,128]{2,1,0:T(8,128)S(1)} %all-to-all-done.r_ref, f32[16,72,128]{2,1,0:T(8,128)S(1)} %get-tuple-element.14.aug_ref, f32[4,72,128]{2,1,0:T(8,128)S(1)} %get-tuple-element.15.sup_ref, ...), custom_call_target="tpu_custom_call" | custom-call | tf_op jit(solution)/shard_map/apply/pallas_call | solution.py:430
  47.1 16.7 %all_to_all.15 = f32[128,2,128]{2,1,0:T(2,128)S(1)} all-to-all(f32[128,2,128]{2,1,0:T(2,128)S(1)} %bitcast.27), channel_id=1, replica_groups=mesh['seq'=4,'tm'=32] {'seq','tm'}, dimensions={0} | all-to-all | bytes 262144 | tf_op jit(solution)/shard_map/all_to_all | solution.py:451
  63.7 0.1 reduce_sum.9
  63.9 14.3 %all_to_all.16 = f32[128,2,128]{2,1,0:T(2,128)S(1)} all-to-all(f32[128,2,128]{2,1,0:T(2,128)S(1)} %broadcast_in_dim.14), channel_id=1, replica_groups=mesh['seq'=4,'tm'=32] {'seq','tm'}, dimensions={0} | all-to-all | bytes 262144 | tf_op jit(solution)/shard_map/all_to_all | solution.py:454
  78.2 0.1 fusion.1
  78.3 0.7 pad_maximum_fusion
  78.9 0.6 slice_bitcast_fusion
  (3 shorter events, 0.1 us)
Async XLA Ops:
  0.6 0.7 copy-start.8
  1.3 0.8 %copy-start = (f32[1,256,64]{1,2,0:T(8,128)S(1)}, f32[1,256,64]{1,2,0:T(8,128)}, u32[]{:S(2)}) copy-start(f32[1,256,64]{1,2,0:T(8,128)} %param.6) | copy-start | bytes 196612
  2.2 0.8 %copy-start.2 = (f32[1,256,64]{1,2,0:T(8,128)S(1)}, f32[1,256,64]{1,2,0:T(8,128)}, u32[]{:S(2)}) copy-start(f32[1,256,64]{1,2,0:T(8,128)} %param.7) | copy-start | bytes 196612
  3.0 0.8 %copy-start.4 = (f32[64,192]{1,0:T(8,128)S(1)}, f32[64,192]{1,0:T(8,128)}, u32[]{:S(2)}) copy-start(f32[64,192]{1,0:T(8,128)} %wh_ref.3) | copy-start | bytes 147460
  3.8 0.8 %copy-start.6 = (f32[1,256,64]{1,2,0:T(8,128)S(1)}, f32[1,256,64]{1,2,0:T(8,128)}, u32[]{:S(2)}) copy-start(f32[1,256,64]{1,2,0:T(8,128)} %param.8) | copy-start | bytes 196612
  4.7 0.8 %copy-start.7 = (f32[64,192]{1,0:T(8,128)S(1)}, f32[64,192]{1,0:T(8,128)}, u32[]{:S(2)}) copy-start(f32[64,192]{1,0:T(8,128)} %wi_ref.1) | copy-start | bytes 147460
  16.2 21.6 %copy-start.1 = (f32[1,256,64]{1,2,0:T(8,128)S(1)}, f32[1,256,64]{1,2,0:T(8,128)}, u32[]{:S(2)}) copy-start(f32[1,256,64]{1,2,0:T(8,128)} %param.6) | copy-start | bytes 196612
  16.2 21.6 %copy-start.3 = (f32[1,256,64]{1,2,0:T(8,128)S(1)}, f32[1,256,64]{1,2,0:T(8,128)}, u32[]{:S(2)}) copy-start(f32[1,256,64]{1,2,0:T(8,128)} %param.7) | copy-start | bytes 196612
  16.2 21.6 %copy-start.5 = (f32[64,192]{1,0:T(8,128)S(1)}, f32[64,192]{1,0:T(8,128)}, u32[]{:S(2)}) copy-start(f32[64,192]{1,0:T(8,128)} %wh_ref.3) | copy-start | bytes 147460
  16.2 21.6 %all-to-all-start = ((f32[32,40,128]{2,1,0:T(8,128)}), f32[32,40,128]{2,1,0:T(8,128)S(1)}, u32[]{:S(2)}, u32[]{:S(2)}) async-start(f32[32,40,128]{2,1,0:T(8,128)} %get-tuple-element.13), calls=%async_computation | async-start | bytes 1310720 | tf_op jit(solution)/shard_map/all_to_all | solution.py:428

commit v2 on v1

--- a/solution.py
+++ b/solution.py
@@ -17,6 +17,7 @@
 DEV = 32
 HALF = DEV // 2
 TILE = 40
+GROUP = 2
 VMEM_LIMIT = 48 * 1024 * 1024
 
 
@@ -54,6 +55,25 @@
     )
     high, low = split(wide)
     return jnp.concatenate([high, high, low], axis=0)
+
+
+def side_weights(wh):
+    n, r, z = [split(doubled(wh[:, k:k + H])) for k in (128, 0, 64)]
+    zero = jnp.zeros((128, 128), BF16)
+    top = jnp.concatenate([n[0], r[0], z[0], n[1]], axis=1)
+    bottom = jnp.concatenate([n[0], r[0], z[0], zero], axis=1)
+    return jnp.concatenate([top, bottom], axis=0), jnp.concatenate([r[1], z[1]], axis=1)
+
+
+def halves(value):
+    return jnp.concatenate(split(value), axis=1)
+
+
+def gates_of(first, second):
+    return (
+        first[:, :128] + first[:, 384:], first[:, 128:256] + second[:, :128],
+        first[:, 256:384] + second[:, 128:],
+    )
 
 
 def backward_weights(wh):
@@ -102,13 +122,26 @@
     )
 
 
+def fetch(pairs, sems):
+    copies = [pltpu.make_async_copy(a, b, sems.at[k]) for k, (a, b) in enumerate(pairs)]
+    for copy in copies:
+        copy.start()
+    return copies
+
+
 def blocks_kernel(
-    x_ref, g_ref, c_ref, wi_ref, wh_ref, bias_ref,
+    x_hbm, g_hbm, c_hbm, wi_hbm, wh_hbm, bias_hbm,
     send_ref, aug_ref, sup_ref, pk_ref, tl_ref,
-    y_ref, z_ref, b_ref, lhs_ref, w_ref,
+    y_ref, z_ref, b_ref, lhs_ref, w1_ref, w2_ref,
+    x_ref, g_ref, c_ref, wi_ref, wh_ref, bias_ref, sems,
 ):
+    for copy in fetch(
+        [(wh_hbm, wh_ref), (g_hbm, g_ref), (wi_hbm, wi_ref), (x_hbm, x_ref), (bias_hbm, bias_ref),
+         (c_hbm, c_ref)], sems,
+    ):
+        copy.wait()
     wh = wh_ref[...]
-    w_ref[...] = forward_weights(wh)
+    w1_ref[...], w2_ref[...] = side_weights(wh)
     guess = g_ref[...]
     prev = pltpu.roll(guess, 1, 1)
     gi = dot(wi_ref[...], x_ref[...], ((0,), (0,)))
@@ -144,15 +177,12 @@
 
     def put(c, value, cot):
         y_ref[c] = value
-        high, low = split(value)
-        lhs_ref[c * H:(c + 1) * H, 0:128] = high
-        lhs_ref[c * H:(c + 1) * H, 128:256] = low
-        lhs_ref[c * H:(c + 1) * H, 256:384] = high
+        lhs_ref[c * H:(c + 1) * H, :] = halves(value)
         return value * cot
 
     def put_b(value):
         b_ref[...] = value
-        lhs_ref[512:528, :] = three(jnp.concatenate([value, jnp.zeros_like(value)], axis=0))
+        lhs_ref[512:528, :] = halves(jnp.concatenate([value, jnp.zeros_like(value)], axis=0))
 
     p0, q0, w0, u0, s0, c0 = [rows(k, 0) for k in range(6)]
     for c in range(PAIRS):
@@ -164,19 +194,23 @@
 
     def step(l, carry):
         p1, q1, w1, u1, s1, c1 = [rows(k, l) for k in range(6)]
-        prod = bdot(lhs_ref[...], w_ref[...])
         for c in range(PAIRS):
-            part = prod[c * H:(c + 1) * H]
+            if c % GROUP == 0:
+                lhs = lhs_ref[c * H:(c + GROUP) * H, :]
+                first, second = bdot(lhs, w1_ref[...]), bdot(lhs[:, :128], w2_ref[...])
+            part = slice((c % GROUP) * H, (c % GROUP + 1) * H)
+            n, r, z = gates_of(first[part], second[part])
             value = (
-                u1[c:c + 1] * y_ref[c] + p1[c:c + 1] * part[:, :128]
-                + q1[c:c + 1] * part[:, 128:256] + w1[c:c + 1] * part[:, 256:]
+                u1[c:c + 1] * y_ref[c] + p1[c:c + 1] * n + q1[c:c + 1] * r + w1[c:c + 1] * z
             )
             z_ref[c] += put(c, value, c1[c:c + 1])
-        part = prod[512:520]
-        put_b(u1 * b_ref[...] + p1 * part[:, :128] + q1 * part[:, 128:256] + w1 * part[:, 256:] + s1)
+        lhs = lhs_ref[512:528, :]
+        first, second = bdot(lhs, w1_ref[...]), bdot(lhs[:, :128], w2_ref[...])
+        n, r, z = gates_of(first[:8], second[:8])
+        put_b(u1 * b_ref[...] + p1 * n + q1 * r + w1 * z + s1)
         return carry
 
-    lax.fori_loop(1, RUN, step, 0)
+    lax.fori_loop(1, RUN, step, 0, unroll=True)
 
     low8 = iota((8, 128), 1) < H
     top8 = iota((8, 128), 0) == 0
@@ -213,25 +247,31 @@
     row_zn = to_row(head(gi_z), 0) + to_row(head(gi_n), H)
     row8 = iota((8, 128), 0)
     tail = jnp.where(row8 == 0, row_bc, jnp.where(row8 == 1, row_gr, jnp.where(row8 == 2, row_zn, 0.0)))
-    for k in range(DEV):
+    for k in range(HALF):
         send_ref[k, 0:32, :] = body
         send_ref[k, 32:40, :] = tail
 
 
 def apply_kernel(
-    me_ref, r_ref, aug_ref, sup_ref, pk_ref, tl_ref, x_ref, g_ref, wh_ref, bias_ref,
+    me_ref, own_ref, other_ref, aug_ref, sup_ref, pk_ref, tl_ref, x_hbm, g_hbm, wh_hbm, bias_hbm,
     state_ref, adj_ref, grad_ref,
     w_ref, wt_ref, lhs_ref, z_ref, d_ref, row_ref, bnd_ref, st_ref, lam_ref,
+    x_ref, g_ref, wh_ref, bias_ref, sems,
 ):
+    copies = fetch([(wh_hbm, wh_ref), (bias_hbm, bias_ref), (g_hbm, g_ref), (x_hbm, x_ref)], sems)
     me = me_ref[0]
+    core = me % 2
+    for k in range(3):
+        row_ref[k, pl.ds(core, HALF, stride=2), :] = own_ref[:, 32 + k, :]
+        row_ref[k, pl.ds(1 - core, HALF, stride=2), :] = other_ref[:, 32 + k, :]
+    for copy in copies:
+        copy.wait()
     wh = wh_ref[...]
     w_ref[...] = forward_weights(wh)
     wt_ref[...] = backward_weights(wh)
     bias_h = bias_ref[1:2, 64:]
 
-    bc = r_ref[:, 32, :]
-    gr = r_ref[:, 33, :]
-    zn = r_ref[:, 34, :]
+    bc, gr, zn = row_ref[0], row_ref[1], row_ref[2]
     prev = jnp.where(iota((DEV, H), 0) == DEV - 1, 0.0, gr[:, :H])
     gr_next = pltpu.roll(gr, DEV - 1, 0)
     zn_next = pltpu.roll(zn, DEV - 1, 0)
@@ -243,7 +283,6 @@
     for k in range(6):
         bnd_ref[k] = jnp.concatenate([terms[k], terms[k]], axis=1)
     bnd_ref[6] = jnp.concatenate([prev, prev], axis=1)
-    row_ref[...] = bc
 
     def pair(a):
         return jnp.concatenate([a[:HALF], a[HALF:]], axis=1)
@@ -252,13 +291,15 @@
     lane64 = iota((H, 128), 1)
     row64 = iota((H, 128), 0)
     low32 = iota((32, 128), 1) < H
-    for k in range(HALF):
-        a, b = r_ref[k, 0:32, :], r_ref[k + HALF, 0:32, :]
-        top = jnp.where(low32, a, pltpu.roll(b, H, 1))
-        bottom = jnp.where(low32, pltpu.roll(a, H, 1), b)
-        value = jnp.concatenate([top, bottom], axis=0)
-        z_ref[k] = value
-        lhs_ref[k * H:(k + 1) * H, :] = three(value)
+    for ref, side in ((own_ref, core), (other_ref, 1 - core)):
+        for k in range(HALF // 2):
+            a, b = ref[k, 0:32, :], ref[k + HALF // 2, 0:32, :]
+            top = jnp.where(low32, a, pltpu.roll(b, H, 1))
+            bottom = jnp.where(low32, pltpu.roll(a, H, 1), b)
+            value = jnp.concatenate([top, bottom], axis=0)
+            z_ref[2 * k + side] = value
+            start = pl.multiple_of((2 * k + side) * H, H)
+            lhs_ref[pl.ds(start, H), :] = three(value)
     offs = pair(bc[:, :H])
     lhs_ref[HALF * H:, :] = three(offs)
     prod = bdot(lhs_ref[...], w_ref[...])
@@ -290,13 +331,13 @@
         def lap(i, lam):
             k = base - i
             col = jnp.sum(z_ref[k % HALF] * lam, axis=1, keepdims=True)
-            extra = row_ref[pl.ds(k, 1), :]
+            extra = row_ref[0, pl.ds(k, 1), :]
             if turn:
                 extra = pltpu.roll(extra, H, 1)
             return jnp.sum(jnp.where(eye, col, 0.0), axis=0, keepdims=True) + jnp.where(keep, extra, 0.0)
         return lap
 
-    lam = jnp.where(lane1 >= H, row_ref[DEV - 1:DEV, :], 0.0)
+    lam = jnp.where(lane1 >= H, row_ref[0, DEV - 1:DEV, :], 0.0)
     lam = lax.fori_loop(
         0, DEV - 1 - jnp.maximum(me + 1, HALF), bwd(eye_b, DEV - 2, False, lane1 >= H), lam
     )
@@ -405,32 +446,46 @@
     g = jnp.swapaxes(guess[0], 0, 1)
     c = jnp.swapaxes(cotangent[0], 0, 1)
     bias2 = bias.reshape(2, 128)
+    x, g, c, w_input, w_hidden, bias2 = [
+        pltpu.with_memory_space_constraint(a, pltpu.HBM)
+        for a in (x, g, c, w_input, w_hidden, bias2)
+    ]
     vmem = pl.BlockSpec(memory_space=pltpu.VMEM)
+    hbm = pl.BlockSpec(memory_space=pltpu.HBM)
+    wide = [pltpu.VMEM((H, T), F32)] * 3
     params = pltpu.CompilerParams(vmem_limit_bytes=VMEM_LIMIT)
     send, aug, sup, pk, tl = pl.pallas_call(
         blocks_kernel,
         out_shape=(
-            shape(DEV, TILE, 128), shape(16, 72, 128), shape(4, 72, 128),
+            shape(HALF, TILE, 128), shape(16, 72, 128), shape(4, 72, 128),
             shape(6, 128, 128), shape(4, H, T),
         ),
-        in_specs=[vmem] * 6,
+        in_specs=[hbm] * 6,
         out_specs=[vmem] * 5,
         scratch_shapes=[
             pltpu.VMEM((PAIRS, H, 128), F32),
             pltpu.VMEM((PAIRS, H, 128), F32),
             pltpu.VMEM((8, 128), F32),
-            pltpu.VMEM((528, 384), BF16),
-            pltpu.VMEM((384, 384), BF16),
+            pltpu.VMEM((528, 256), BF16),
+            pltpu.VMEM((256, 512), BF16),
+            pltpu.VMEM((128, 256), BF16),
+        ] + wide + [
+            pltpu.VMEM((H, 192), F32),
+            pltpu.VMEM((H, 192), F32),
+            pltpu.VMEM((2, 128), F32),
+            pltpu.SemaphoreType.DMA((6,)),
         ],
         compiler_params=params,
         name="blocks",
     )(x, g, c, w_input, w_hidden, bias2)
-    received = lax.all_to_all(send, "tm", 0, 0)
+    groups = [[2 * k + core for k in range(HALF)] for core in range(2)]
+    received = lax.all_to_all(send, "tm", 0, 0, axis_index_groups=groups)
+    other = lax.ppermute(received, "tm", [(k, k ^ 1) for k in range(DEV)])
     me = lax.axis_index("tm").astype(jnp.int32).reshape(1)
     states, adjoint, grads = pl.pallas_call(
         apply_kernel,
         out_shape=(shape(H, T), shape(H, T), shape(256, 128)),
-        in_specs=[pl.BlockSpec(memory_space=pltpu.SMEM)] + [vmem] * 9,
+        in_specs=[pl.BlockSpec(memory_space=pltpu.SMEM)] + [vmem] * 6 + [hbm] * 4,
         out_specs=[vmem] * 3,
         scratch_shapes=[
             pltpu.VMEM((384, 384), BF16),
@@ -438,14 +493,18 @@
             pltpu.VMEM((HALF * H + 16, 384), BF16),
             pltpu.VMEM((HALF, H, 128), F32),
             pltpu.VMEM((HALF, 128), F32),
-            pltpu.VMEM((DEV, 128), F32),
+            pltpu.VMEM((3, DEV, 128), F32),
             pltpu.VMEM((7, DEV, 128), F32),
             pltpu.VMEM((128, 128), F32),
             pltpu.VMEM((128, 128), F32),
+        ] + wide[:2] + [
+            pltpu.VMEM((H, 192), F32),
+            pltpu.VMEM((2, 128), F32),
+            pltpu.SemaphoreType.DMA((4,)),
         ],
         compiler_params=params,
         name="apply",
-    )(me, received, aug, sup, pk, tl, x, g, w_hidden, bias2)
+    )(me, received, other, aug, sup, pk, tl, x, g, w_hidden, bias2)
     axes = ("seq", "tm")
     count = lax.axis_size("seq") * lax.axis_size("tm")
     pieces = lax.all_to_all(grads.reshape(count, 2, 128), axes, 0, 0)

time: 80 us -> 70.3 us (0.88)
  blocking collectives: 30.9 us -> 46.4 us
  waiting for transfers between devices: 12.9 us -> 1.26 us
  starting transfers between devices: 8.72 us -> 1.88 us
  local copies, waits for them, and re-layouts: 5.56 us -> 0.68 us
  Pallas kernels: 19.9 us -> 18.3 us
    all_to_all x0 -> x1, blocking collectives: none -> 15.8 us  [per_device(): received = lax.all_to_all(send, 'tm', 0, 0, axis_index_groups=groups)]
    all_to_all x1 -> x0, waiting for transfers between devices: 12.9 us -> none  [per_device(): received = lax.all_to_all(send, 'tm', 0, 0)]
    all_to_all x1 -> x0, starting transfers between devices: 8.72 us -> none  [per_device(): received = lax.all_to_all(send, 'tm', 0, 0)]
    unnamed x18 -> x0, local copies, waits for them, and re-layouts: 4.88 us -> none
    pallas_call x1, Pallas kernels: 10.6 us -> 7.93 us  [per_device(): pl.pallas_call(blocks_kernel, out_shape=(shape(HALF, TILE, 128), shape(16...]
    ppermute x0 -> x1, starting transfers between devices: none -> 1.88 us  [per_device(): other = lax.ppermute(received, 'tm', [(k, k ^ 1) for k in range(DEV)])]
    ppermute x0 -> x1, waiting for transfers between devices: none -> 1.26 us  [per_device(): other = lax.ppermute(received, 'tm', [(k, k ^ 1) for k in range(DEV)])]
    pallas_call x1, Pallas kernels: 9.26 us -> 10.4 us  [per_device(): pl.pallas_call(apply_kernel, out_shape=(shape(H, T), shape(H, T), shape(2...]
where the time goes in v2:
time: 70.3 us; the launch traced here: 70 us
  blocking collectives  46.4 us (66%)
  Pallas kernels  18.3 us (26%)
  starting transfers between devices  1.88 us (3%)
  waiting for transfers between devices  1.26 us (2%)
  other arithmetic  0.81 us (1%)
    all_to_all x1, blocking collectives, per_device(): pieces = lax.all_to_all(grads.reshape(count, 2, 128), axes, 0, 0)  16.3 us
    all_to_all x1, blocking collectives, per_device(): received = lax.all_to_all(send, 'tm', 0, 0, axis_index_groups=groups)  15.8 us
    all_to_all x1, blocking collectives, per_device(): lax.all_to_all(jnp.broadcast_to(mine[None], (count, 2, 128)), axes, 0, 0)  14.3 us
    pallas_call x1, Pallas kernels, per_device(): pl.pallas_call(apply_kernel, out_shape=(shape(H, T), shape(H, T), shape(2...  10.4 us
    pallas_call x1, Pallas kernels, per_device(): pl.pallas_call(blocks_kernel, out_shape=(shape(HALF, TILE, 128), shape(16...  7.93 us
    ppermute x1, starting transfers between devices, per_device(): other = lax.ppermute(received, 'tm', [(k, k ^ 1) for k in range(DEV)])  1.88 us
  transfers between devices with their start and end apart: 1, of which 1 were waited for; matrix products, arithmetic and copies ran while one was open for 0% of the time, Pallas kernels for 0%

profile of v2, /device:TPU:1, one launch (start us, length us, event | category | flops | bytes accessed | tf_op | source)
XLA Modules:
  0.0 70.0 jit_solution(9887727093041485168)
XLA Ops:
  0.6 7.9 %blocks.1 = (f32[16,40,128]{2,1,0:T(8,128)S(1)}, f32[16,72,128]{2,1,0:T(8,128)S(1)}, f32[4,72,128]{2,1,0:T(8,128)S(1)}, f32[6,128,128]{2,1,0:T(8,128)S(1)}, f32[4,64,256]{2,1,0:T(8,128)S(1)}) custom-call(f32[64,256]{1,0:T(8,128)} %bitcast.25, f32[64,256]{1,0:T(8,128)} %bitcast.27, f32[64,256]{1,0:T(8,128)} %bitcast.31, f32[64,192]{1,0:T(8,128)} %wi_hbm.1, ...), custom_call_target="tpu_custom_call" | custom-call | tf_op jit(solution)/shard_map/blocks/pallas_call | solution.py:457
  8.6 15.8 %all_to_all.15.own_ref = f32[16,40,128]{2,1,0:T(8,128)S(1)} all-to-all(f32[16,40,128]{2,1,0:T(8,128)S(1)} %get-tuple-element.13), channel_id=1, replica_groups={{0,2,4,6,8,10,12,14,16,18,20,22,24,26,28,30},{1,3,5,7,9,11,13,15,17,19,..., dimensions={0} | all-to-all | bytes 655360 | tf_op jit(solution)/shard_map/all_to_all | solution.py:482
  24.4 1.9 %collective-permute-start = (f32[16,40,128]{2,1,0:T(8,128)S(1)}, f32[16,40,128]{2,1,0:T(8,128)S(1)}, u32[]{:S(2)}, u32[]{:S(2)}) collective-permute-start(f32[16,40,128]{2,1,0:T(8,128)S(1)} %all_to_all.15.own_ref), channel_id=1, source_target_pairs={{0,1},{1,0},{2,3},{3,2},{4,5},{5,4},{6,7},{7,6},{8,9},{9,8},{10,11... | collective-permute-start | bytes 983048 | tf_op jit(solution)/shard_map/ppermute | solution.py:483
  26.3 1.3 %collective-permute-done.other_ref = f32[16,40,128]{2,1,0:T(8,128)S(1)} collective-permute-done((f32[16,40,128]{2,1,0:T(8,128)S(1)}, f32[16,40,128]{2,1,0:T(8,128)S(1)}, u32[]{:S(2)}, u32[]{:S(2)}) %collective-permute-start) | collective-permute-done | bytes 327712 | tf_op jit(solution)/shard_map/ppermute | solution.py:483
  27.5 10.4 %apply.1 = (f32[64,256]{1,0:T(8,128)}, f32[64,256]{1,0:T(8,128)}, f32[256,128]{1,0:T(8,128)S(1)}) custom-call(s32[1]{0:T(128)} %bitcast.me_ref, f32[16,40,128]{2,1,0:T(8,128)S(1)} %all_to_all.15.own_ref, f32[16,40,128]{2,1,0:T(8,128)S(1)} %collective-permute-done.other_ref, f32[16,72,128]{2,1,0:T(8,128)S(1)} %get-tuple-element.14.aug_ref, ...), custom_call_target="tpu_custom_call" | custom-call | tf_op jit(solution)/shard_map/apply/pallas_call | solution.py:485
  38.0 16.3 %all_to_all.16 = f32[128,2,128]{2,1,0:T(2,128)S(1)} all-to-all(f32[128,2,128]{2,1,0:T(2,128)S(1)} %bitcast.23), channel_id=1, replica_groups=mesh['seq'=4,'tm'=32] {'seq','tm'}, dimensions={0} | all-to-all | bytes 262144 | tf_op jit(solution)/shard_map/all_to_all | solution.py:510
  54.3 0.1 reduce_sum.9
  54.5 14.3 %all_to_all.17 = f32[128,2,128]{2,1,0:T(2,128)S(1)} all-to-all(f32[128,2,128]{2,1,0:T(2,128)S(1)} %broadcast_in_dim.14), channel_id=1, replica_groups=mesh['seq'=4,'tm'=32] {'seq','tm'}, dimensions={0} | all-to-all | bytes 262144 | tf_op jit(solution)/shard_map/all_to_all | solution.py:513
  68.7 0.1 fusion.1
  68.8 0.7 pad_maximum_fusion
  69.5 0.6 slice_bitcast_fusion
  (3 shorter events, 0.0 us)
Async XLA Ops:
  24.4 3.1 %collective-permute-start = (f32[16,40,128]{2,1,0:T(8,128)S(1)}, f32[16,40,128]{2,1,0:T(8,128)S(1)}, u32[]{:S(2)}, u32[]{:S(2)}) collective-permute-start(f32[16,40,128]{2,1,0:T(8,128)S(1)} %all_to_all.15.own_ref), channel_id=1, source_target_pairs={{0,1},{1,0},{2,3},{3,2},{4,5},{5,4},{6,7},{7,6},{8,9},{9,8},{10,11... | collective-permute-start | bytes 983048 | tf_op jit(solution)/shard_map/ppermute | solution.py:483

commit v3 on v2

--- a/solution.py
+++ b/solution.py
@@ -49,14 +49,6 @@
     )
 
 
-def forward_weights(wh):
-    wide = jnp.concatenate(
-        [doubled(wh[:, 128:192]), doubled(wh[:, :64]), doubled(wh[:, 64:128])], axis=1
-    )
-    high, low = split(wide)
-    return jnp.concatenate([high, high, low], axis=0)
-
-
 def side_weights(wh):
     n, r, z = [split(doubled(wh[:, k:k + H])) for k in (128, 0, 64)]
     zero = jnp.zeros((128, 128), BF16)
@@ -77,16 +69,30 @@
 
 
 def backward_weights(wh):
-    tall = jnp.concatenate(
-        [doubled(wh[:, 128:192].T), doubled(wh[:, :64].T), doubled(wh[:, 64:128].T)], axis=0
-    )
-    high, low = split(tall)
-    return jnp.concatenate([high, high, low], axis=0)
-
-
-def three(a):
-    high, low = split(a)
-    return jnp.concatenate([high, low, high], axis=1)
+    tall = jnp.concatenate([doubled(wh[:, k:k + H].T) for k in (128, 0, 64)], axis=0)
+    return jnp.concatenate(split(tall), axis=1)
+
+
+def stacked(value):
+    high = value.astype(BF16).astype(F32)
+    return jnp.concatenate([high, value - high], axis=0).astype(BF16)
+
+
+def narrow_gates(value, w1_ref, w2_ref):
+    rows = value.shape[0]
+    weights = jnp.concatenate([w1_ref[:128, :], w2_ref[...]], axis=1)
+    out = bdot(stacked(value), weights)
+    high, low = out[:rows], out[rows:]
+    n = high[:, :128] + high[:, 384:512] + low[:, :128]
+    r = high[:, 128:256] + high[:, 512:640] + low[:, 128:256]
+    z = high[:, 256:384] + high[:, 640:] + low[:, 256:384]
+    return n, r, z
+
+
+def pulled(mixed, wt_ref):
+    rows = mixed.shape[0]
+    out = bdot(stacked(mixed), wt_ref[...])
+    return out[:rows, :128] + out[rows:, :128] + out[:rows, 128:]
 
 
 def to_row(column, offset):
@@ -131,8 +137,8 @@
 
 def blocks_kernel(
     x_hbm, g_hbm, c_hbm, wi_hbm, wh_hbm, bias_hbm,
-    send_ref, aug_ref, sup_ref, pk_ref, tl_ref,
-    y_ref, z_ref, b_ref, lhs_ref, w1_ref, w2_ref,
+    send_ref, aug_ref, sup_ref, pk_ref, tl_ref, w1_ref, w2_ref, wt_ref, hb_ref,
+    y_ref, z_ref, b_ref, lhs_ref,
     x_ref, g_ref, c_ref, wi_ref, wh_ref, bias_ref, sems,
 ):
     for copy in fetch(
@@ -142,6 +148,9 @@
         copy.wait()
     wh = wh_ref[...]
     w1_ref[...], w2_ref[...] = side_weights(wh)
+    wt_ref[...] = backward_weights(wh)
+    hb = jnp.broadcast_to(bias_ref[1:2, :], (8, 128))
+    hb_ref[...] = jnp.where(iota((8, 128), 1) < H, pltpu.roll(hb, H, 1), hb)
     guess = g_ref[...]
     prev = pltpu.roll(guess, 1, 1)
     gi = dot(wi_ref[...], x_ref[...], ((0,), (0,)))
@@ -253,41 +262,38 @@
 
 
 def apply_kernel(
-    me_ref, own_ref, other_ref, aug_ref, sup_ref, pk_ref, tl_ref, x_hbm, g_hbm, wh_hbm, bias_hbm,
+    me_ref, own_ref, other_ref, aug_ref, sup_ref, pk_ref, tl_ref, w1_ref, w2_ref, wt_ref, hb_ref,
+    x_hbm, g_hbm,
     state_ref, adj_ref, grad_ref,
-    w_ref, wt_ref, lhs_ref, z_ref, d_ref, row_ref, bnd_ref, st_ref, lam_ref,
-    x_ref, g_ref, wh_ref, bias_ref, sems,
+    lhs_ref, z_ref, zt_ref, row_ref, bnd_ref, st_ref, lam_ref, x_ref, g_ref, sems,
 ):
-    copies = fetch([(wh_hbm, wh_ref), (bias_hbm, bias_ref), (g_hbm, g_ref), (x_hbm, x_ref)], sems)
+    copies = fetch([(g_hbm, g_ref), (x_hbm, x_ref)], sems)
     me = me_ref[0]
     core = me % 2
     for k in range(3):
         row_ref[k, pl.ds(core, HALF, stride=2), :] = own_ref[:, 32 + k, :]
         row_ref[k, pl.ds(1 - core, HALF, stride=2), :] = other_ref[:, 32 + k, :]
-    for copy in copies:
-        copy.wait()
-    wh = wh_ref[...]
-    w_ref[...] = forward_weights(wh)
-    wt_ref[...] = backward_weights(wh)
-    bias_h = bias_ref[1:2, 64:]
-
     bc, gr, zn = row_ref[0], row_ref[1], row_ref[2]
-    prev = jnp.where(iota((DEV, H), 0) == DEV - 1, 0.0, gr[:, :H])
+    low16 = iota((HALF, 128), 1) < H
+
+    def pair_low(a):
+        return jnp.where(low16, a[:HALF], pltpu.roll(a[HALF:], H, 1))
+
+    def pair_high(a):
+        return jnp.where(low16, pltpu.roll(a[:HALF], H, 1), a[HALF:])
+
     gr_next = pltpu.roll(gr, DEV - 1, 0)
     zn_next = pltpu.roll(zn, DEV - 1, 0)
-    gh = dot(prev, wh)
+    prev = jnp.where((iota((HALF, 128), 0) == HALF - 1) & ~low16, 0.0, pair_low(gr))
+    n, r, z = narrow_gates(prev, w1_ref, w2_ref)
     terms = gate_terms(
-        gr_next[:, H:], zn_next[:, :H], zn_next[:, H:],
-        gh[:, :64], gh[:, 64:128], gh[:, 128:], bias_h, prev,
+        pair_high(gr_next), pair_low(zn_next), pair_high(zn_next), r, z, n, hb_ref[0:1, :], prev
     )
     for k in range(6):
-        bnd_ref[k] = jnp.concatenate([terms[k], terms[k]], axis=1)
-    bnd_ref[6] = jnp.concatenate([prev, prev], axis=1)
-
-    def pair(a):
-        return jnp.concatenate([a[:HALF], a[HALF:]], axis=1)
-
-    p, q, w, u, shift = [pair(terms[k]) for k in (1, 2, 3, 4, 5)]
+        bnd_ref[k] = terms[k]
+    bnd_ref[6] = prev
+    squash, p, q, w, u, shift = terms
+
     lane64 = iota((H, 128), 1)
     row64 = iota((H, 128), 0)
     low32 = iota((32, 128), 1) < H
@@ -299,58 +305,78 @@
             value = jnp.concatenate([top, bottom], axis=0)
             z_ref[2 * k + side] = value
             start = pl.multiple_of((2 * k + side) * H, H)
-            lhs_ref[pl.ds(start, H), :] = three(value)
-    offs = pair(bc[:, :H])
-    lhs_ref[HALF * H:, :] = three(offs)
-    prod = bdot(lhs_ref[...], w_ref[...])
+            lhs_ref[pl.ds(start, H), :] = halves(value)
+    offs = pair_low(bc)
+    lhs_ref[HALF * H:, :] = halves(offs)
     for k in range(HALF):
-        part = prod[k * H:(k + 1) * H]
-        z_ref[k] = (
-            u[k:k + 1] * z_ref[k] + p[k:k + 1] * part[:, :128]
-            + q[k:k + 1] * part[:, 128:256] + w[k:k + 1] * part[:, 256:]
-        )
-    part = prod[HALF * H:]
-    d_ref[...] = u * offs + p * part[:, :128] + q * part[:, 128:256] + w * part[:, 256:] + shift
+        if k % GROUP == 0:
+            lhs = lhs_ref[k * H:(k + GROUP) * H, :]
+            first, second = bdot(lhs, w1_ref[...]), bdot(lhs[:, :128], w2_ref[...])
+        part = slice((k % GROUP) * H, (k % GROUP + 1) * H)
+        n, r, z = gates_of(first[part], second[part])
+        value = u[k:k + 1] * z_ref[k] + p[k:k + 1] * n + q[k:k + 1] * r + w[k:k + 1] * z
+        z_ref[k] = value
+        if k % 2:
+            zt_ref[k // 2] = jnp.concatenate([value, pltpu.roll(value, H, 1)], axis=0).T[:H]
+    lhs = lhs_ref[HALF * H:, :]
+    n, r, z = gates_of(bdot(lhs, w1_ref[...]), bdot(lhs[:, :128], w2_ref[...]))
+    fwd_rows = u * offs + p * n + q * r + w * z + shift
+    bwd_rows = pair_high(bc)
+    empty = jnp.zeros((128 - HALF, 128), F32)
+    fwd_cols = jnp.concatenate([fwd_rows, empty], axis=0).T
+    bwd_cols = jnp.concatenate([bwd_rows, empty], axis=0).T
 
     lane1 = iota((1, 128), 1)
+    low1 = lane1 < H
     eye_a = lane64 == row64
     eye_b = lane64 == row64 + H
-
-    def fwd(eye, base):
-        def lap(k, x):
-            col = jnp.sum(jnp.where(eye, x, 0.0), axis=1, keepdims=True)
-            return jnp.sum(col * z_ref[k - base], axis=0, keepdims=True) + d_ref[pl.ds(k - base, 1), :]
-        return lap
-
-    x = bnd_ref[5, DEV - 1:DEV, :]
-    x = lax.fori_loop(0, jnp.minimum(me, HALF), fwd(eye_a, 0), x)
-    x = lax.fori_loop(HALF, me, fwd(eye_b, HALF), pltpu.roll(x, H, 1))
-    x = pltpu.roll(x, H, 1)
-
-    def bwd(eye, base, turn, keep):
-        def lap(i, lam):
-            k = base - i
-            col = jnp.sum(z_ref[k % HALF] * lam, axis=1, keepdims=True)
-            extra = row_ref[0, pl.ds(k, 1), :]
-            if turn:
-                extra = pltpu.roll(extra, H, 1)
-            return jnp.sum(jnp.where(eye, col, 0.0), axis=0, keepdims=True) + jnp.where(keep, extra, 0.0)
-        return lap
-
-    lam = jnp.where(lane1 >= H, row_ref[0, DEV - 1:DEV, :], 0.0)
-    lam = lax.fori_loop(
-        0, DEV - 1 - jnp.maximum(me + 1, HALF), bwd(eye_b, DEV - 2, False, lane1 >= H), lam
-    )
-    lam = lax.fori_loop(
-        0, jnp.maximum(HALF - 1 - me, 0), bwd(eye_a, HALF - 1, True, lane1 < H), pltpu.roll(lam, H, 1)
-    )
-    row_terms = [bnd_ref[k, pl.ds(me, 1), :] for k in range(6)]
-    lam8 = jnp.broadcast_to(lam, (8, 128))[:, :H]
-    wide = jnp.concatenate([lam8 * row_terms[k][:, :H] for k in (1, 2, 3)], axis=1)
-    tall = jnp.concatenate([wh[:, 128:192].T, wh[:, :64].T, wh[:, 64:128].T], axis=0)
-    carry = (dot(wide, tall) + lam8 * row_terms[4][:, :H])[0:1]
-    carry = jnp.where(me == DEV - 1, 0.0, carry)
-    carry = jnp.concatenate([carry, jnp.zeros_like(carry)], axis=1)
+    shift_last = shift[HALF - 1:HALF, :]
+    x_col = jnp.sum(jnp.where(eye_b, shift_last, 0.0), axis=1, keepdims=True)
+    lam_row = jnp.where(low1, 0.0, bwd_rows[HALF - 1:HALF, :])
+    zero_col, zero_row = jnp.zeros((H, 1), F32), jnp.zeros((1, 128), F32)
+    x_keep = jnp.where(me == 0, x_col, zero_col)
+    lam_keep = zero_col
+    x_rows, lam_rows = zero_row, jnp.where(me + 1 == DEV - 1, lam_row, zero_row)
+
+    def half(k, row):
+        return jnp.where(low1, row, 0.0) if k < HALF else jnp.where(low1, 0.0, row)
+
+    def side_cols(cols, k):
+        return jnp.where(lane64 == k % HALF, cols[:H] if k < HALF else cols[H:], 0.0)
+
+    for i in range(DEV - 1):
+        k, m = i, i % HALF
+        if k % 2 == 0:
+            x_row = half(k, jnp.sum(x_col * z_ref[m], axis=0, keepdims=True) + fwd_rows[m:m + 1])
+            x_rows = jnp.where(me == k + 1, x_row, x_rows)
+        else:
+            x_col = jnp.sum(zt_ref[m // 2] * x_row + side_cols(fwd_cols, k), axis=1, keepdims=True)
+            x_keep = jnp.where(me == k + 1, x_col, x_keep)
+        k = DEV - 2 - i
+        m = k % HALF
+        if k % 2 == 0:
+            lam_col = jnp.sum(z_ref[m] * lam_row + side_cols(bwd_cols, k), axis=1, keepdims=True)
+            lam_keep = jnp.where(me + 1 == k, lam_col, lam_keep)
+        else:
+            lam_row = half(
+                k, jnp.sum(lam_col * zt_ref[m // 2], axis=0, keepdims=True) + bwd_rows[m:m + 1]
+            )
+            lam_rows = jnp.where(me + 1 == k, lam_row, lam_rows)
+
+    def settled(rows, column):
+        row = jnp.where(low1, rows, 0.0) + jnp.where(low1, pltpu.roll(rows, H, 1), 0.0)
+        return row + jnp.sum(jnp.where(eye_a, column, 0.0), axis=0, keepdims=True)
+
+    x = settled(x_rows, x_keep)
+    lam = settled(lam_rows, lam_keep)
+
+    def boundary(k, index):
+        row = bnd_ref[k, pl.ds(index % HALF, 1), :]
+        return jnp.where(low1, jnp.where(index >= HALF, pltpu.roll(row, H, 1), row), 0.0)
+
+    lam8 = jnp.broadcast_to(lam, (8, 128))
+    mixed = jnp.concatenate([lam8 * boundary(k, me) for k in (1, 2, 3)], axis=1)
+    carry = (pulled(mixed, wt_ref) + lam8 * boundary(4, me))[0:1]
 
     row72 = iota((72, 128), 0)
     eye72 = iota((72, 128), 1) == row72
@@ -389,25 +415,17 @@
     def rows(k, step):
         return pk_ref[k, pl.ds(step, PAIRS, stride=RUN), :]
 
-    def pad(a):
-        return jnp.concatenate([a, jnp.zeros_like(a)], axis=0)
-
-    def lap(i, both):
-        state, kappa = both
+    state, kappa = gather(state_rows), gather(carry_rows)
+    for i in range(RUN):
         j = RUN - 1 - i
-        prod = bdot(three(pad(state)), w_ref[...])[:8]
+        n, r, z = narrow_gates(state, w1_ref, w2_ref)
         lam = rows(5, j) + kappa
         lam_ref[pl.ds(j, PAIRS, stride=RUN), :] = lam
         mixed = jnp.concatenate([lam * rows(0, j), lam * rows(1, j), lam * rows(2, j)], axis=1)
-        kappa = bdot(three(pad(mixed)), wt_ref[...])[:8] + lam * rows(3, j)
-        state = (
-            rows(3, i) * state + rows(0, i) * prod[:, :128] + rows(1, i) * prod[:, 128:256]
-            + rows(2, i) * prod[:, 256:] + rows(4, i)
-        )
+        kappa = pulled(mixed, wt_ref) + lam * rows(3, j)
+        state = rows(3, i) * state + rows(0, i) * n + rows(1, i) * r + rows(2, i) * z + rows(4, i)
         st_ref[pl.ds(i, PAIRS, stride=RUN), :] = state
-        return state, kappa
-
-    lax.fori_loop(0, RUN, lap, (gather(state_rows), gather(carry_rows)))
+
     states = st_ref[...].T
     state_ref[:, :128] = states[:H]
     state_ref[:, 128:] = states[H:]
@@ -419,9 +437,11 @@
     first = iota((H, T), 1) == 0
 
     def with_first(a, k):
-        col = jnp.sum(jnp.where(eye_a, bnd_ref[k, pl.ds(before, 1), :], 0.0), axis=1, keepdims=True)
+        col = jnp.sum(jnp.where(eye_a, boundary(k, before), 0.0), axis=1, keepdims=True)
         return jnp.where(first, col, a)
 
+    for copy in copies:
+        copy.wait()
     squash, p, q, w = [with_first(tl_ref[k], k) for k in range(4)]
     prev = with_first(pltpu.roll(g_ref[...], 1, 1), 6)
     left = jnp.concatenate([x_ref[...], prev, jnp.ones((8, T), F32)], axis=0)
@@ -454,21 +474,21 @@
     hbm = pl.BlockSpec(memory_space=pltpu.HBM)
     wide = [pltpu.VMEM((H, T), F32)] * 3
     params = pltpu.CompilerParams(vmem_limit_bytes=VMEM_LIMIT)
-    send, aug, sup, pk, tl = pl.pallas_call(
+    send, *kept = pl.pallas_call(
         blocks_kernel,
         out_shape=(
             shape(HALF, TILE, 128), shape(16, 72, 128), shape(4, 72, 128),
             shape(6, 128, 128), shape(4, H, T),
+            jax.ShapeDtypeStruct((256, 512), BF16), jax.ShapeDtypeStruct((128, 256), BF16),
+            jax.ShapeDtypeStruct((384, 256), BF16), shape(8, 128),
         ),
         in_specs=[hbm] * 6,
-        out_specs=[vmem] * 5,
+        out_specs=[vmem] * 9,
         scratch_shapes=[
             pltpu.VMEM((PAIRS, H, 128), F32),
             pltpu.VMEM((PAIRS, H, 128), F32),
             pltpu.VMEM((8, 128), F32),
             pltpu.VMEM((528, 256), BF16),
-            pltpu.VMEM((256, 512), BF16),
-            pltpu.VMEM((128, 256), BF16),
         ] + wide + [
             pltpu.VMEM((H, 192), F32),
             pltpu.VMEM((H, 192), F32),
@@ -485,26 +505,20 @@
     states, adjoint, grads = pl.pallas_call(
         apply_kernel,
         out_shape=(shape(H, T), shape(H, T), shape(256, 128)),
-        in_specs=[pl.BlockSpec(memory_space=pltpu.SMEM)] + [vmem] * 6 + [hbm] * 4,
+        in_specs=[pl.BlockSpec(memory_space=pltpu.SMEM)] + [vmem] * 10 + [hbm] * 2,
         out_specs=[vmem] * 3,
         scratch_shapes=[
-            pltpu.VMEM((384, 384), BF16),
-            pltpu.VMEM((1152, 128), BF16),
-            pltpu.VMEM((HALF * H + 16, 384), BF16),
+            pltpu.VMEM((HALF * H + 16, 256), BF16),
             pltpu.VMEM((HALF, H, 128), F32),
-            pltpu.VMEM((HALF, 128), F32),
+            pltpu.VMEM((HALF // 2, H, 128), F32),
             pltpu.VMEM((3, DEV, 128), F32),
-            pltpu.VMEM((7, DEV, 128), F32),
+            pltpu.VMEM((7, HALF, 128), F32),
             pltpu.VMEM((128, 128), F32),
             pltpu.VMEM((128, 128), F32),
-        ] + wide[:2] + [
-            pltpu.VMEM((H, 192), F32),
-            pltpu.VMEM((2, 128), F32),
-            pltpu.SemaphoreType.DMA((4,)),
-        ],
+        ] + wide[:2] + [pltpu.SemaphoreType.DMA((2,))],
         compiler_params=params,
         name="apply",
-    )(me, received, other, aug, sup, pk, tl, x, g, w_hidden, bias2)
+    )(me, received, other, *kept, x, g)
     axes = ("seq", "tm")
     count = lax.axis_size("seq") * lax.axis_size("tm")
     pieces = lax.all_to_all(grads.reshape(count, 2, 128), axes, 0, 0)

time: 70.3 us -> 66.9 us (0.952)
  Pallas kernels: 18.3 us -> 14.9 us
    pallas_call x1, Pallas kernels: 10.4 us -> 6.89 us  [per_device(): pl.pallas_call(apply_kernel, out_shape=(shape(H, T), shape(H, T), shape(2...]
where the time goes in v3:
time: 66.9 us; the launch traced here: 66.7 us
  blocking collectives  46.4 us (69%)
  Pallas kernels  14.9 us (22%)
  starting transfers between devices  1.87 us (3%)
  waiting for transfers between devices  1.26 us (2%)
  other arithmetic  0.81 us (1%)
  local copies, waits for them, and re-layouts  0.68 us (1%)
    all_to_all x1, blocking collectives, per_device(): pieces = lax.all_to_all(grads.reshape(count, 2, 128), axes, 0, 0)  16.3 us
    all_to_all x1, blocking collectives, per_device(): received = lax.all_to_all(send, 'tm', 0, 0, axis_index_groups=groups)  15.9 us
    all_to_all x1, blocking collectives, per_device(): lax.all_to_all(jnp.broadcast_to(mine[None], (count, 2, 128)), axes, 0, 0)  14.3 us
    pallas_call x1, Pallas kernels, per_device(): pl.pallas_call(blocks_kernel, out_shape=(shape(HALF, TILE, 128), shape(16...  8.05 us
    pallas_call x1, Pallas kernels, per_device(): pl.pallas_call(apply_kernel, out_shape=(shape(H, T), shape(H, T), shape(2...  6.89 us
    ppermute x1, starting transfers between devices, per_device(): other = lax.ppermute(received, 'tm', [(k, k ^ 1) for k in range(DEV)])  1.87 us
  transfers between devices with their start and end apart: 1, of which 1 were waited for; matrix products, arithmetic and copies ran while one was open for 0% of the time, Pallas kernels for 0%

profile of v3, /device:TPU:1, one launch (start us, length us, event | category | flops | bytes accessed | tf_op | source)
XLA Modules:
  0.0 66.7 jit_solution(14225844839481028390)
XLA Ops:
  0.6 8.1 %blocks.1 = (f32[16,40,128]{2,1,0:T(8,128)S(1)}, f32[16,72,128]{2,1,0:T(8,128)S(1)}, f32[4,72,128]{2,1,0:T(8,128)S(1)}, f32[6,128,128]{2,1,0:T(8,128)S(1)}, f32[...) custom-call(f32[64,256]{1,0:T(8,128)} %bitcast.25, ...), custom_call_target="tpu_custom_call" | custom-call | tf_op jit(solution)/shard_map/blocks/pallas_call | solution.py:477
  8.7 15.9 %all_to_all.15.own_ref = f32[16,40,128]{2,1,0:T(8,128)S(1)} all-to-all(f32[16,40,128]{2,1,0:T(8,128)S(1)} %get-tuple-element.17), channel_id=1, replica_groups={{0,2,4,6,8,10,12,14,16,18,20,22,24,26,28,30},{1,3,5,7,9,11,13,15,17,19,..., dimensions={0} | all-to-all | bytes 655360 | tf_op jit(solution)/shard_map/all_to_all | solution.py:502
  24.6 1.9 %collective-permute-start = (f32[16,40,128]{2,1,0:T(8,128)S(1)}, f32[16,40,128]{2,1,0:T(8,128)S(1)}, u32[]{:S(2)}, u32[]{:S(2)}) collective-permute-start(f32[16,40,128]{2,1,0:T(8,128)S(1)} %all_to_all.15.own_ref), channel_id=1, source_target_pairs={{0,1},{1,0},{2,3},{3,2},{4,5},{5,4},{6,7},{7,6},{8,9},{9,8},{10,11... | collective-permute-start | bytes 983048 | tf_op jit(solution)/shard_map/ppermute | solution.py:503
  26.4 1.3 %collective-permute-done.other_ref = f32[16,40,128]{2,1,0:T(8,128)S(1)} collective-permute-done((f32[16,40,128]{2,1,0:T(8,128)S(1)}, f32[16,40,128]{2,1,0:T(8,128)S(1)}, u32[]{:S(2)}, u32[]{:S(2)}) %collective-permute-start) | collective-permute-done | bytes 327712 | tf_op jit(solution)/shard_map/ppermute | solution.py:503
  27.7 6.9 %apply.1 = (f32[64,256]{1,0:T(8,128)}, f32[64,256]{1,0:T(8,128)}, f32[256,128]{1,0:T(8,128)S(1)}) custom-call(s32[1]{0:T(128)} %bitcast.me_ref, f32[16,40,128]{2,1,0:T(8,128)S(1)} %all_to_all.15.own_ref, f32[16,40,128]{2,1,0:T(8,128)S(1)} %collective-permute-done.other_ref, f32[16,72,128]{2,1,0:T(8,128)S(1)} %get-tuple-element.18.aug_ref, ...), custom_call_target="tpu_custom_call" | custom-call | tf_op jit(solution)/shard_map/apply/pallas_call | solution.py:505
  34.6 16.3 %all_to_all.16 = f32[128,2,128]{2,1,0:T(2,128)S(1)} all-to-all(f32[128,2,128]{2,1,0:T(2,128)S(1)} %bitcast.23), channel_id=1, replica_groups=mesh['seq'=4,'tm'=32] {'seq','tm'}, dimensions={0} | all-to-all | bytes 262144 | tf_op jit(solution)/shard_map/all_to_all | solution.py:524
  50.9 0.1 reduce_sum.9
  51.1 14.3 %all_to_all.17 = f32[128,2,128]{2,1,0:T(2,128)S(1)} all-to-all(f32[128,2,128]{2,1,0:T(2,128)S(1)} %broadcast_in_dim.14), channel_id=1, replica_groups=mesh['seq'=4,'tm'=32] {'seq','tm'}, dimensions={0} | all-to-all | bytes 262144 | tf_op jit(solution)/shard_map/all_to_all | solution.py:527
  65.4 0.1 fusion.1
  65.4 0.7 pad_maximum_fusion
  66.1 0.6 slice_bitcast_fusion
  (3 shorter events, 0.1 us)
Async XLA Ops:
  24.6 3.1 %collective-permute-start = (f32[16,40,128]{2,1,0:T(8,128)S(1)}, f32[16,40,128]{2,1,0:T(8,128)S(1)}, u32[]{:S(2)}, u32[]{:S(2)}) collective-permute-start(f32[16,40,128]{2,1,0:T(8,128)S(1)} %all_to_all.15.own_ref), channel_id=1, source_target_pairs={{0,1},{1,0},{2,3},{3,2},{4,5},{5,4},{6,7},{7,6},{8,9},{9,8},{10,11... | collective-permute-start | bytes 983048 | tf_op jit(solution)/shard_map/ppermute | solution.py:503

commit v4 on v3

--- a/solution.py
+++ b/solution.py
@@ -1,3 +1,4 @@
+import functools
 import math
 
 import jax
@@ -18,6 +19,7 @@
 HALF = DEV // 2
 TILE = 40
 GROUP = 2
+PART = 104
 VMEM_LIMIT = 48 * 1024 * 1024
 
 
@@ -264,8 +266,9 @@
 def apply_kernel(
     me_ref, own_ref, other_ref, aug_ref, sup_ref, pk_ref, tl_ref, w1_ref, w2_ref, wt_ref, hb_ref,
     x_hbm, g_hbm,
-    state_ref, adj_ref, grad_ref,
+    state_hbm, adj_hbm, keep_ref, give_ref,
     lhs_ref, z_ref, zt_ref, row_ref, bnd_ref, st_ref, lam_ref, x_ref, g_ref, sems,
+    state_ref, adj_ref, out_sems,
 ):
     copies = fetch([(g_hbm, g_ref), (x_hbm, x_ref)], sems)
     me = me_ref[0]
@@ -432,6 +435,7 @@
     lams = lam_ref[...].T
     lams = jnp.concatenate([lams[:H], lams[H:]], axis=1)
     adj_ref[...] = lams
+    results = fetch([(state_ref, state_hbm), (adj_ref, adj_hbm)], out_sems)
 
     before = (me + DEV - 1) % DEV
     first = iota((H, T), 1) == 0
@@ -447,18 +451,53 @@
     left = jnp.concatenate([x_ref[...], prev, jnp.ones((8, T), F32)], axis=0)
     right = jnp.concatenate([lams * q, lams * w, lams * squash, lams * p], axis=0)
     sums = dot(left, right, ((1,), (1,)))
-    grad_ref[0:64, :] = sums[:64, :128]
-    grad_ref[64:128, :] = sums[64:128, :128]
-    grad_ref[128:192, :] = jnp.where(lane64 < H, sums[:64, 128:], sums[64:128, 128:])
     row8 = iota((8, 128), 0)
-    grad_ref[192:200, :] = jnp.where(
+    biases = jnp.where(
         row8 == 0, sums[128:136, :128], jnp.where(row8 == 1, sums[128:136, 128:], 0.0)
     )
-    grad_ref[200:, :] = jnp.zeros((56, 128), F32)
+    last = jnp.where(lane64 < H, sums[:64, 128:], sums[64:128, 128:])
+    first_half = sums[:PART, :128]
+    second_half = jnp.concatenate([sums[PART:128, :128], last, biases, jnp.zeros((8, 128), F32)], axis=0)
+    keep_ref[...] = jnp.where(core == 0, first_half, second_half)
+    give_ref[...] = jnp.where(core == 0, second_half, first_half)
+    for copy in results:
+        copy.wait()
+
+
+def finish_kernel(me_ref, own_ref, other_ref, gin_ref, ghid_ref, gbias_ref, *, scale):
+    core = me_ref[0] % 2
+    own, other = own_ref[...] * scale, other_ref[...] * scale
+    whole = jnp.concatenate(
+        [jnp.where(core == 0, own, other), jnp.where(core == 0, other, own)], axis=0
+    )
+    gin_ref[:, :128] = whole[:64]
+    gin_ref[:, 128:] = whole[128:192, :64]
+    ghid_ref[:, :128] = whole[64:128]
+    ghid_ref[:, 128:] = whole[128:192, 64:]
+    gbias_ref[...] = whole[192:194]
 
 
 def shape(*dims):
     return jax.ShapeDtypeStruct(dims, F32)
+
+
+def swapped(a):
+    return lax.ppermute(a, "tm", [(k, k ^ 1) for k in range(DEV)])
+
+
+def grouped(members):
+    found = {}
+    for z in range(4):
+        for y in range(4):
+            for x in range(4):
+                for core in range(2):
+                    place = z * DEV + y * 8 + x * 2 + core
+                    found.setdefault(members(z, y, x, core), []).append(place)
+    return list(found.values())
+
+
+AROUND = grouped(lambda z, y, x, core: (z, y // 2, core))
+ACROSS = grouped(lambda z, y, x, core: (y % 2, x, core))
 
 
 def per_device(inputs, guess, cotangent, w_input, w_hidden, bias):
@@ -472,6 +511,7 @@
     ]
     vmem = pl.BlockSpec(memory_space=pltpu.VMEM)
     hbm = pl.BlockSpec(memory_space=pltpu.HBM)
+    smem = pl.BlockSpec(memory_space=pltpu.SMEM)
     wide = [pltpu.VMEM((H, T), F32)] * 3
     params = pltpu.CompilerParams(vmem_limit_bytes=VMEM_LIMIT)
     send, *kept = pl.pallas_call(
@@ -500,13 +540,13 @@
     )(x, g, c, w_input, w_hidden, bias2)
     groups = [[2 * k + core for k in range(HALF)] for core in range(2)]
     received = lax.all_to_all(send, "tm", 0, 0, axis_index_groups=groups)
-    other = lax.ppermute(received, "tm", [(k, k ^ 1) for k in range(DEV)])
+    other = swapped(received)
     me = lax.axis_index("tm").astype(jnp.int32).reshape(1)
-    states, adjoint, grads = pl.pallas_call(
+    states, adjoint, part, give = pl.pallas_call(
         apply_kernel,
-        out_shape=(shape(H, T), shape(H, T), shape(256, 128)),
-        in_specs=[pl.BlockSpec(memory_space=pltpu.SMEM)] + [vmem] * 10 + [hbm] * 2,
-        out_specs=[vmem] * 3,
+        out_shape=(shape(H, T), shape(H, T), shape(PART, 128), shape(PART, 128)),
+        in_specs=[smem] + [vmem] * 10 + [hbm] * 2,
+        out_specs=[hbm] * 2 + [vmem] * 2,
         scratch_shapes=[
             pltpu.VMEM((HALF * H + 16, 256), BF16),
             pltpu.VMEM((HALF, H, 128), F32),
@@ -515,20 +555,25 @@
             pltpu.VMEM((7, HALF, 128), F32),
             pltpu.VMEM((128, 128), F32),
             pltpu.VMEM((128, 128), F32),
-        ] + wide[:2] + [pltpu.SemaphoreType.DMA((2,))],
+        ] + wide[:2] + [pltpu.SemaphoreType.DMA((2,))] + wide[:2] + [pltpu.SemaphoreType.DMA((2,))],
         compiler_params=params,
         name="apply",
     )(me, received, other, *kept, x, g)
+    part = part + swapped(give)
     axes = ("seq", "tm")
-    count = lax.axis_size("seq") * lax.axis_size("tm")
-    pieces = lax.all_to_all(grads.reshape(count, 2, 128), axes, 0, 0)
+    for group in (AROUND, ACROSS):
+        copies = jnp.broadcast_to(part[None], (8, PART, 128))
+        part = jnp.sum(lax.all_to_all(copies, axes, 0, 0, axis_index_groups=group), axis=0)
     scale = 1.0 / math.sqrt(lax.axis_size("seq") * lax.axis_size("tm") * T)
-    mine = jnp.sum(pieces, axis=0) * scale
-    whole = lax.all_to_all(jnp.broadcast_to(mine[None], (count, 2, 128)), axes, 0, 0)
-    whole = whole.reshape(256, 128)
-    grad_input = jnp.concatenate([whole[0:64], whole[128:192, :64]], axis=1)
-    grad_hidden = jnp.concatenate([whole[64:128], whole[128:192, 64:]], axis=1)
-    grad_bias = whole[192:194].reshape(256)
+    grad_input, grad_hidden, grad_bias = pl.pallas_call(
+        functools.partial(finish_kernel, scale=scale),
+        out_shape=(shape(H, 192), shape(H, 192), shape(2, 128)),
+        in_specs=[smem, vmem, vmem],
+        out_specs=[vmem] * 3,
+        compiler_params=params,
+        name="finish",
+    )(me, part, swapped(part))
+    grad_bias = grad_bias.reshape(256)
     return (
         jnp.swapaxes(states, 0, 1)[None], jnp.swapaxes(adjoint, 0, 1)[None],
         grad_input, grad_hidden, grad_bias,

time: 66.9 us -> 66.2 us (0.990)
  blocking collectives: 46.4 us -> 41.2 us
  starting transfers between devices: 1.87 us -> 5.28 us
  waiting for transfers between devices: 1.26 us -> 3.03 us
  other arithmetic: 0.81 us -> 0.06 us
  Pallas kernels: 14.9 us -> 15.6 us
    all_to_all x2, blocking collectives: 30.6 us -> 25.3 us  [per_device(): lax.all_to_all(copies, axes, 0, 0, axis_index_groups=group)]
    ppermute x1 -> x3, starting transfers between devices: 1.87 us -> 5.28 us  [swapped(): return lax.ppermute(a, 'tm', [(k, k ^ 1) for k in range(DEV)])]
    ppermute x1 -> x3, waiting for transfers between devices: 1.26 us -> 3.03 us  [swapped(): return lax.ppermute(a, 'tm', [(k, k ^ 1) for k in range(DEV)])]
    pallas_call x1 -> x2, Pallas kernels: 6.89 us -> 7.53 us  [the longest x1 6.82 us: per_device(): pl.pallas_call(apply_kernel, out_shape=(shape(H, T), shape(H, T), shape(P...]
  transfers between devices with their start and end apart: 1 -> 3, of which waited for: 1 -> 3; matrix products, arithmetic and copies ran while one was open for 0% -> 0% of each run, Pallas kernels for 0% -> 0%
where the time goes in v4:
time: 66.2 us; the launch traced here: 65.9 us
  blocking collectives  41.2 us (62%)
  Pallas kernels  15.6 us (24%)
  starting transfers between devices  5.28 us (8%)
  waiting for transfers between devices  3.03 us (5%)
  between operations  0.67 us (1%)
    all_to_all x2, blocking collectives, per_device(): lax.all_to_all(copies, axes, 0, 0, axis_index_groups=group)  25.3 us
    all_to_all x1, blocking collectives, per_device(): received = lax.all_to_all(send, 'tm', 0, 0, axis_index_groups=groups)  15.9 us
    pallas_call x1, Pallas kernels, per_device(): pl.pallas_call(blocks_kernel, out_shape=(shape(HALF, TILE, 128), shape(16...  8.05 us
    pallas_call x1, Pallas kernels, per_device(): pl.pallas_call(apply_kernel, out_shape=(shape(H, T), shape(H, T), shape(P...  6.82 us
    ppermute x3, starting transfers between devices, swapped(): return lax.ppermute(a, 'tm', [(k, k ^ 1) for k in range(DEV)])  5.28 us
    ppermute x3, waiting for transfers between devices, swapped(): return lax.ppermute(a, 'tm', [(k, k ^ 1) for k in range(DEV)])  3.03 us
  transfers between devices with their start and end apart: 3, of which 3 were waited for; matrix products, arithmetic and copies ran while one was open for 0% of the time, Pallas kernels for 0%

profile of v4, /device:TPU:1, one launch (start us, length us, event | category | flops | bytes accessed | tf_op | source)
XLA Modules:
  0.0 65.9 jit_solution(7700962980347545672)
XLA Ops:
  0.6 8.1 %blocks.1 = (f32[16,40,128]{2,1,0:T(8,128)S(1)}, f32[16,72,128]{2,1,0:T(8,128)S(1)}, f32[4,72,128]{2,1,0:T(8,128)S(1)}, f32[6,128,128]{2,1,0:T(8,128)S(1)}, f32[...) custom-call(f32[64,256]{1,0:T(8,128)} %bitcast.18, ...), custom_call_target="tpu_custom_call" | custom-call | tf_op jit(solution)/shard_map/blocks/pallas_call | solution.py:517
  8.7 15.9 %all_to_all.15.own_ref = f32[16,40,128]{2,1,0:T(8,128)S(1)} all-to-all(f32[16,40,128]{2,1,0:T(8,128)S(1)} %get-tuple-element.21), channel_id=1, replica_groups={{0,2,4,6,8,10,12,14,16,18,20,22,24,26,28,30},{1,3,5,7,9,11,13,15,17,19,..., dimensions={0} | all-to-all | bytes 655360 | tf_op jit(solution)/shard_map/all_to_all | solution.py:542
  24.6 1.9 %collective-permute-start = (f32[16,40,128]{2,1,0:T(8,128)S(1)}, f32[16,40,128]{2,1,0:T(8,128)S(1)}, u32[]{:S(2)}, u32[]{:S(2)}) collective-permute-start(f32[16,40,128]{2,1,0:T(8,128)S(1)} %all_to_all.15.own_ref), channel_id=1, source_target_pairs={{0,1},{1,0},{2,3},{3,2},{4,5},{5,4},{6,7},{7,6},{8,9},{9,8},{10,11... | collective-permute-start | bytes 983048 | tf_op jit(solution)/shard_map/ppermute | solution.py:485
  26.4 1.3 %collective-permute-done.other_ref = f32[16,40,128]{2,1,0:T(8,128)S(1)} collective-permute-done((f32[16,40,128]{2,1,0:T(8,128)S(1)}, f32[16,40,128]{2,1,0:T(8,128)S(1)}, u32[]{:S(2)}, u32[]{:S(2)}) %collective-permute-start) | collective-permute-done | bytes 327712 | tf_op jit(solution)/shard_map/ppermute | solution.py:485
  27.7 6.8 %apply.1 = (f32[64,256]{1,0:T(8,128)}, f32[64,256]{1,0:T(8,128)}, f32[104,128]{1,0:T(8,128)S(1)}, f32[104,128]{1,0:T(8,128)S(1)}) custom-call(s32[1]{0:T(128)} %bitcast.me_ref, f32[16,40,128]{2,1,0:T(8,128)S(1)} %all_to_all.15.own_ref, f32[16,40,128]{2,1,0:T(8,128)S(1)} %collective-permute-done.other_ref, f32[16,72,128]{2,1,0:T(8,128)S(1)} %get-tuple-element.22.aug_ref, ...), custom_call_target="tpu_custom_call" | custom-call | tf_op jit(solution)/shard_map/apply/pallas_call | solution.py:545
  34.5 0.5 collective-permute-start.1
  35.0 0.9 %collective-permute-done.1 = f32[104,128]{1,0:T(8,128)S(1)} collective-permute-done((f32[104,128]{1,0:T(8,128)S(1)}, f32[104,128]{1,0:T(8,128)S(1)}, u32[]{:S(2)}, u32[]{:S(2)}) %collective-permute-start.1) | collective-permute-done | bytes 53280 | tf_op jit(solution)/shard_map/ppermute | solution.py:485
  35.9 11.0 %all_to_all.16 = f32[8,104,128]{2,1,0:T(8,128)S(1)} all-to-all(f32[8,104,128]{2,1,0:T(8,128)S(1)} %broadcast_in_dim.20), channel_id=1, replica_groups={{0,2,4,6,8,10,12,14},{1,3,5,7,9,11,13,15},{16,18,20,22,24,26,28,30},{17..., dimensions={0} | all-to-all | bytes 851968 | tf_op jit(solution)/shard_map/all_to_all | solution.py:566
  47.0 14.3 %all_to_all.17 = f32[8,104,128]{2,1,0:T(8,128)S(1)} all-to-all(f32[8,104,128]{2,1,0:T(8,128)S(1)} %broadcast_in_dim.21), channel_id=1, replica_groups={{0,16,32,48,64,80,96,112},{1,17,33,49,65,81,97,113},{2,18,34,50,66,82,9..., dimensions={0} | all-to-all | bytes 851968 | tf_op jit(solution)/shard_map/all_to_all | solution.py:566
  61.3 3.0 %collective-permute-start.2 = (f32[104,128]{1,0:T(8,128)S(1)}, f32[104,128]{1,0:T(8,128)S(1)}, u32[]{:S(2)}, u32[]{:S(2)}) collective-permute-start(f32[104,128]{1,0:T(8,128)S(1)} %reduce_sum.19.own_ref), channel_id=1, source_target_pairs={{0,1},{1,0},{2,3},{3,2},{4,5},{5,4},{6,7},{7,6},{8,9},{9,8},{10,11... | collective-permute-start | bytes 159752 | tf_op jit(solution)/shard_map/ppermute | solution.py:485
  64.3 0.9 %collective-permute-done.2.other_ref = f32[104,128]{1,0:T(8,128)S(1)} collective-permute-done((f32[104,128]{1,0:T(8,128)S(1)}, f32[104,128]{1,0:T(8,128)S(1)}, u32[]{:S(2)}, u32[]{:S(2)}) %collective-permute-start.2) | collective-permute-done | bytes 53280 | tf_op jit(solution)/shard_map/ppermute | solution.py:485
  65.2 0.7 %finish.1 = (f32[64,192]{1,0:T(8,128)}, f32[64,192]{1,0:T(8,128)}, f32[2,128]{1,0:T(2,128)}) custom-call(s32[1]{0:T(128)} %bitcast.me_ref, f32[104,128]{1,0:T(8,128)S(1)} %reduce_sum.19.own_ref, f32[104,128]{1,0:T(8,128)S(1)} %collective-permute-done.2.other_ref), custom_call_target="tpu_custom_call" | custom-call | tf_op jit(solution)/shard_map/finish/pallas_call | solution.py:568
  (5 shorter events, 0.1 us)
Async XLA Ops:
  24.6 3.1 %collective-permute-start = (f32[16,40,128]{2,1,0:T(8,128)S(1)}, f32[16,40,128]{2,1,0:T(8,128)S(1)}, u32[]{:S(2)}, u32[]{:S(2)}) collective-permute-start(f32[16,40,128]{2,1,0:T(8,128)S(1)} %all_to_all.15.own_ref), channel_id=1, source_target_pairs={{0,1},{1,0},{2,3},{3,2},{4,5},{5,4},{6,7},{7,6},{8,9},{9,8},{10,11... | collective-permute-start | bytes 983048 | tf_op jit(solution)/shard_map/ppermute | solution.py:485
  34.5 1.3 %collective-permute-start.1 = (f32[104,128]{1,0:T(8,128)S(1)}, f32[104,128]{1,0:T(8,128)S(1)}, u32[]{:S(2)}, u32[]{:S(2)}) collective-permute-start(f32[104,128]{1,0:T(8,128)S(1)} %get-tuple-element.33), channel_id=1, source_target_pairs={{0,1},{1,0},{2,3},{3,2},{4,5},{5,4},{6,7},{7,6},{8,9},{9,8},{10,11... | collective-permute-start | bytes 159752 | tf_op jit(solution)/shard_map/ppermute | solution.py:485
  61.3 3.8 %collective-permute-start.2 = (f32[104,128]{1,0:T(8,128)S(1)}, f32[104,128]{1,0:T(8,128)S(1)}, u32[]{:S(2)}, u32[]{:S(2)}) collective-permute-start(f32[104,128]{1,0:T(8,128)S(1)} %reduce_sum.19.own_ref), channel_id=1, source_target_pairs={{0,1},{1,0},{2,3},{3,2},{4,5},{5,4},{6,7},{7,6},{8,9},{9,8},{10,11... | collective-permute-start | bytes 159752 | tf_op jit(solution)/shard_map/ppermute | solution.py:485

commit v5 on v4

--- a/solution.py
+++ b/solution.py
@@ -122,7 +122,8 @@
 
 def combine(earlier, later):
     row, lane = iota((72, 128), 0), iota((72, 128), 1)
-    product = dot(earlier[:, :H], later[:H, :])
+    out = bdot(stacked(earlier[:, :H]), jnp.concatenate(split(later[:H, :]), axis=1))
+    product = out[:72, :128] + out[72:, :128] + out[:72, 128:]
     return (
         product
         + jnp.where((lane == H) & (row < H), earlier, 0.0)

time: 66.2 us -> 65.7 us (level)
  no operation moved by 1% of the time
where the time goes in v5:
time: 65.7 us; the launch traced here: 65.4 us
  blocking collectives  41.2 us (63%)
  Pallas kernels  15.1 us (23%)
  starting transfers between devices  5.28 us (8%)
  waiting for transfers between devices  3.03 us (5%)
  between operations  0.67 us (1%)
    all_to_all x2, blocking collectives, per_device(): lax.all_to_all(copies, axes, 0, 0, axis_index_groups=group)  25.3 us
    all_to_all x1, blocking collectives, per_device(): received = lax.all_to_all(send, 'tm', 0, 0, axis_index_groups=groups)  15.9 us
    pallas_call x1, Pallas kernels, per_device(): pl.pallas_call(blocks_kernel, out_shape=(shape(HALF, TILE, 128), shape(16...  7.55 us
    pallas_call x1, Pallas kernels, per_device(): pl.pallas_call(apply_kernel, out_shape=(shape(H, T), shape(H, T), shape(P...  6.83 us
    ppermute x3, starting transfers between devices, swapped(): return lax.ppermute(a, 'tm', [(k, k ^ 1) for k in range(DEV)])  5.28 us
    ppermute x3, waiting for transfers between devices, swapped(): return lax.ppermute(a, 'tm', [(k, k ^ 1) for k in range(DEV)])  3.03 us
  transfers between devices with their start and end apart: 3, of which 3 were waited for; matrix products, arithmetic and copies ran while one was open for 0% of the time, Pallas kernels for 0%

profile of v5, /device:TPU:1, one launch (start us, length us, event | category | flops | bytes accessed | tf_op | source)
XLA Modules:
  0.0 65.4 jit_solution(12129072220522560644)
XLA Ops:
  0.6 7.5 %blocks.1 = (f32[16,40,128]{2,1,0:T(8,128)S(1)}, f32[16,72,128]{2,1,0:T(8,128)S(1)}, f32[4,72,128]{2,1,0:T(8,128)S(1)}, f32[6,128,128]{2,1,0:T(8,128)S(1)}, f32[...) custom-call(f32[64,256]{1,0:T(8,128)} %bitcast.18, ...), custom_call_target="tpu_custom_call" | custom-call | tf_op jit(solution)/shard_map/blocks/pallas_call | solution.py:518
  8.2 15.9 %all_to_all.15.own_ref = f32[16,40,128]{2,1,0:T(8,128)S(1)} all-to-all(f32[16,40,128]{2,1,0:T(8,128)S(1)} %get-tuple-element.21), channel_id=1, replica_groups={{0,2,4,6,8,10,12,14,16,18,20,22,24,26,28,30},{1,3,5,7,9,11,13,15,17,19,..., dimensions={0} | all-to-all | bytes 655360 | tf_op jit(solution)/shard_map/all_to_all | solution.py:543
  24.0 1.9 %collective-permute-start = (f32[16,40,128]{2,1,0:T(8,128)S(1)}, f32[16,40,128]{2,1,0:T(8,128)S(1)}, u32[]{:S(2)}, u32[]{:S(2)}) collective-permute-start(f32[16,40,128]{2,1,0:T(8,128)S(1)} %all_to_all.15.own_ref), channel_id=1, source_target_pairs={{0,1},{1,0},{2,3},{3,2},{4,5},{5,4},{6,7},{7,6},{8,9},{9,8},{10,11... | collective-permute-start | bytes 983048 | tf_op jit(solution)/shard_map/ppermute | solution.py:486
  25.9 1.3 %collective-permute-done.other_ref = f32[16,40,128]{2,1,0:T(8,128)S(1)} collective-permute-done((f32[16,40,128]{2,1,0:T(8,128)S(1)}, f32[16,40,128]{2,1,0:T(8,128)S(1)}, u32[]{:S(2)}, u32[]{:S(2)}) %collective-permute-start) | collective-permute-done | bytes 327712 | tf_op jit(solution)/shard_map/ppermute | solution.py:486
  27.2 6.8 %apply.1 = (f32[64,256]{1,0:T(8,128)}, f32[64,256]{1,0:T(8,128)}, f32[104,128]{1,0:T(8,128)S(1)}, f32[104,128]{1,0:T(8,128)S(1)}) custom-call(s32[1]{0:T(128)} %bitcast.me_ref, f32[16,40,128]{2,1,0:T(8,128)S(1)} %all_to_all.15.own_ref, f32[16,40,128]{2,1,0:T(8,128)S(1)} %collective-permute-done.other_ref, f32[16,72,128]{2,1,0:T(8,128)S(1)} %get-tuple-element.22.aug_ref, ...), custom_call_target="tpu_custom_call" | custom-call | tf_op jit(solution)/shard_map/apply/pallas_call | solution.py:546
  34.0 0.5 collective-permute-start.1
  34.5 0.9 %collective-permute-done.1 = f32[104,128]{1,0:T(8,128)S(1)} collective-permute-done((f32[104,128]{1,0:T(8,128)S(1)}, f32[104,128]{1,0:T(8,128)S(1)}, u32[]{:S(2)}, u32[]{:S(2)}) %collective-permute-start.1) | collective-permute-done | bytes 53280 | tf_op jit(solution)/shard_map/ppermute | solution.py:486
  35.4 11.0 %all_to_all.16 = f32[8,104,128]{2,1,0:T(8,128)S(1)} all-to-all(f32[8,104,128]{2,1,0:T(8,128)S(1)} %broadcast_in_dim.20), channel_id=1, replica_groups={{0,2,4,6,8,10,12,14},{1,3,5,7,9,11,13,15},{16,18,20,22,24,26,28,30},{17..., dimensions={0} | all-to-all | bytes 851968 | tf_op jit(solution)/shard_map/all_to_all | solution.py:567
  46.5 14.3 %all_to_all.17 = f32[8,104,128]{2,1,0:T(8,128)S(1)} all-to-all(f32[8,104,128]{2,1,0:T(8,128)S(1)} %broadcast_in_dim.21), channel_id=1, replica_groups={{0,16,32,48,64,80,96,112},{1,17,33,49,65,81,97,113},{2,18,34,50,66,82,9..., dimensions={0} | all-to-all | bytes 851968 | tf_op jit(solution)/shard_map/all_to_all | solution.py:567
  60.8 3.0 %collective-permute-start.2 = (f32[104,128]{1,0:T(8,128)S(1)}, f32[104,128]{1,0:T(8,128)S(1)}, u32[]{:S(2)}, u32[]{:S(2)}) collective-permute-start(f32[104,128]{1,0:T(8,128)S(1)} %reduce_sum.19.own_ref), channel_id=1, source_target_pairs={{0,1},{1,0},{2,3},{3,2},{4,5},{5,4},{6,7},{7,6},{8,9},{9,8},{10,11... | collective-permute-start | bytes 159752 | tf_op jit(solution)/shard_map/ppermute | solution.py:486
  63.8 0.9 %collective-permute-done.2.other_ref = f32[104,128]{1,0:T(8,128)S(1)} collective-permute-done((f32[104,128]{1,0:T(8,128)S(1)}, f32[104,128]{1,0:T(8,128)S(1)}, u32[]{:S(2)}, u32[]{:S(2)}) %collective-permute-start.2) | collective-permute-done | bytes 53280 | tf_op jit(solution)/shard_map/ppermute | solution.py:486
  64.7 0.7 %finish.1 = (f32[64,192]{1,0:T(8,128)}, f32[64,192]{1,0:T(8,128)}, f32[2,128]{1,0:T(2,128)}) custom-call(s32[1]{0:T(128)} %bitcast.me_ref, f32[104,128]{1,0:T(8,128)S(1)} %reduce_sum.19.own_ref, f32[104,128]{1,0:T(8,128)S(1)} %collective-permute-done.2.other_ref), custom_call_target="tpu_custom_call" | custom-call | tf_op jit(solution)/shard_map/finish/pallas_call | solution.py:569
  (5 shorter events, 0.1 us)
Async XLA Ops:
  24.0 3.1 %collective-permute-start = (f32[16,40,128]{2,1,0:T(8,128)S(1)}, f32[16,40,128]{2,1,0:T(8,128)S(1)}, u32[]{:S(2)}, u32[]{:S(2)}) collective-permute-start(f32[16,40,128]{2,1,0:T(8,128)S(1)} %all_to_all.15.own_ref), channel_id=1, source_target_pairs={{0,1},{1,0},{2,3},{3,2},{4,5},{5,4},{6,7},{7,6},{8,9},{9,8},{10,11... | collective-permute-start | bytes 983048 | tf_op jit(solution)/shard_map/ppermute | solution.py:486
  34.0 1.3 %collective-permute-start.1 = (f32[104,128]{1,0:T(8,128)S(1)}, f32[104,128]{1,0:T(8,128)S(1)}, u32[]{:S(2)}, u32[]{:S(2)}) collective-permute-start(f32[104,128]{1,0:T(8,128)S(1)} %get-tuple-element.33), channel_id=1, source_target_pairs={{0,1},{1,0},{2,3},{3,2},{4,5},{5,4},{6,7},{7,6},{8,9},{9,8},{10,11... | collective-permute-start | bytes 159752 | tf_op jit(solution)/shard_map/ppermute | solution.py:486
  60.8 3.8 %collective-permute-start.2 = (f32[104,128]{1,0:T(8,128)S(1)}, f32[104,128]{1,0:T(8,128)S(1)}, u32[]{:S(2)}, u32[]{:S(2)}) collective-permute-start(f32[104,128]{1,0:T(8,128)S(1)} %reduce_sum.19.own_ref), channel_id=1, source_target_pairs={{0,1},{1,0},{2,3},{3,2},{4,5},{5,4},{6,7},{7,6},{8,9},{9,8},{10,11... | collective-permute-start | bytes 159752 | tf_op jit(solution)/shard_map/ppermute | solution.py:486

commit v6 on v5

--- a/solution.py
+++ b/solution.py
@@ -486,19 +486,12 @@
     return lax.ppermute(a, "tm", [(k, k ^ 1) for k in range(DEV)])
 
 
-def grouped(members):
-    found = {}
-    for z in range(4):
-        for y in range(4):
-            for x in range(4):
-                for core in range(2):
-                    place = z * DEV + y * 8 + x * 2 + core
-                    found.setdefault(members(z, y, x, core), []).append(place)
-    return list(found.values())
-
-
-AROUND = grouped(lambda z, y, x, core: (z, y // 2, core))
-ACROSS = grouped(lambda z, y, x, core: (y % 2, x, core))
+def summed_by_four(a, axis, stride):
+    count = lax.axis_size(axis)
+    one, two, three_off = [
+        lax.ppermute(a, axis, [(k, k ^ (step * stride)) for k in range(count)]) for step in (1, 2, 3)
+    ]
+    return lax.optimization_barrier((a + one) + (two + three_off))
 
 
 def per_device(inputs, guess, cotangent, w_input, w_hidden, bias):
@@ -561,10 +554,8 @@
         name="apply",
     )(me, received, other, *kept, x, g)
     part = part + swapped(give)
-    axes = ("seq", "tm")
-    for group in (AROUND, ACROSS):
-        copies = jnp.broadcast_to(part[None], (8, PART, 128))
-        part = jnp.sum(lax.all_to_all(copies, axes, 0, 0, axis_index_groups=group), axis=0)
+    for axis, stride in (("seq", 1), ("tm", 8), ("tm", 2)):
+        part = summed_by_four(part, axis, stride)
     scale = 1.0 / math.sqrt(lax.axis_size("seq") * lax.axis_size("tm") * T)
     grad_input, grad_hidden, grad_bias = pl.pallas_call(
         functools.partial(finish_kernel, scale=scale),

time: 65.7 us -> 61.2 us (0.932)
  blocking collectives: 41.2 us -> 15.9 us
  starting transfers between devices: 5.28 us -> 18.2 us
  waiting for transfers between devices: 3.03 us -> 11 us
    all_to_all x2 -> x0, blocking collectives: 25.3 us -> none  [per_device(): lax.all_to_all(copies, axes, 0, 0, axis_index_groups=group)]
    ppermute x0 -> x9, starting transfers between devices: none -> 11.2 us  [summed_by_four(): lax.ppermute(a, axis, [(k, k ^ step * stride) for k in range(count)])]
    ppermute x0 -> x9, waiting for transfers between devices: none -> 7.99 us  [summed_by_four(): lax.ppermute(a, axis, [(k, k ^ step * stride) for k in range(count)])]
    ppermute x3, starting transfers between devices: 5.28 us -> 7.09 us  [swapped(): return lax.ppermute(a, 'tm', [(k, k ^ 1) for k in range(DEV)])]
  transfers between devices with their start and end apart: 3 -> 12, of which waited for: 3 -> 11; matrix products, arithmetic and copies ran while one was open for 0% -> 0% of each run, Pallas kernels for 0% -> 0%
where the time goes in v6:
time: 61.2 us; the launch traced here: 60.9 us
  starting transfers between devices  18.2 us (30%)
  blocking collectives  15.9 us (26%)
  Pallas kernels  15.1 us (25%)
  waiting for transfers between devices  11 us (18%)
  between operations  0.67 us (1%)
    all_to_all x1, blocking collectives, per_device(): received = lax.all_to_all(send, 'tm', 0, 0, axis_index_groups=groups)  15.9 us
    ppermute x9, starting transfers between devices, summed_by_four(): lax.ppermute(a, axis, [(k, k ^ step * stride) for k in range(count)])  11.2 us
    ppermute x9, waiting for transfers between devices, summed_by_four(): lax.ppermute(a, axis, [(k, k ^ step * stride) for k in range(count)])  7.99 us
    pallas_call x1, Pallas kernels, per_device(): pl.pallas_call(blocks_kernel, out_shape=(shape(HALF, TILE, 128), shape(16...  7.55 us
    ppermute x3, starting transfers between devices, swapped(): return lax.ppermute(a, 'tm', [(k, k ^ 1) for k in range(DEV)])  7.09 us
    pallas_call x1, Pallas kernels, per_device(): pl.pallas_call(apply_kernel, out_shape=(shape(H, T), shape(H, T), shape(P...  6.83 us
    ppermute x3, waiting for transfers between devices, swapped(): return lax.ppermute(a, 'tm', [(k, k ^ 1) for k in range(DEV)])  3.03 us
  transfers between devices with their start and end apart: 12, of which 11 were waited for; matrix products, arithmetic and copies ran while one was open for 0% of the time, Pallas kernels for 0%

profile of v6, /device:TPU:1, one launch (start us, length us, event | category | flops | bytes accessed | tf_op | source)
XLA Modules:
  0.0 60.9 jit_solution(13214667171158733484)
XLA Ops:
  0.6 7.5 %blocks.1 = (f32[16,40,128]{2,1,0:T(8,128)S(1)}, f32[16,72,128]{2,1,0:T(8,128)S(1)}, f32[4,72,128]{2,1,0:T(8,128)S(1)}, f32[6,128,128]{2,1,0:T(8,128)S(1)}, f32[...) custom-call(f32[64,256]{1,0:T(8,128)} %bitcast.18, ...), custom_call_target="tpu_custom_call" | custom-call | tf_op jit(solution)/shard_map/blocks/pallas_call | solution.py:511
  8.2 15.9 %all_to_all.5.own_ref = f32[16,40,128]{2,1,0:T(8,128)S(1)} all-to-all(f32[16,40,128]{2,1,0:T(8,128)S(1)} %get-tuple-element.21), channel_id=1, replica_groups={{0,2,4,6,8,10,12,14,16,18,20,22,24,26,28,30},{1,3,5,7,9,11,13,15,17,19,..., dimensions={0} | all-to-all | bytes 655360 | tf_op jit(solution)/shard_map/all_to_all | solution.py:536
  24.0 1.9 %collective-permute-start = (f32[16,40,128]{2,1,0:T(8,128)S(1)}, f32[16,40,128]{2,1,0:T(8,128)S(1)}, u32[]{:S(2)}, u32[]{:S(2)}) collective-permute-start(f32[16,40,128]{2,1,0:T(8,128)S(1)} %all_to_all.5.own_ref), channel_id=1, source_target_pairs={{0,1},{1,0},{2,3},{3,2},{4,5},{5,4},{6,7},{7,6},{8,9},{9,8},{10,11... | collective-permute-start | bytes 983048 | tf_op jit(solution)/shard_map/ppermute | solution.py:486
  25.9 1.3 %collective-permute-done.other_ref = f32[16,40,128]{2,1,0:T(8,128)S(1)} collective-permute-done((f32[16,40,128]{2,1,0:T(8,128)S(1)}, f32[16,40,128]{2,1,0:T(8,128)S(1)}, u32[]{:S(2)}, u32[]{:S(2)}) %collective-permute-start) | collective-permute-done | bytes 327712 | tf_op jit(solution)/shard_map/ppermute | solution.py:486
  27.2 6.8 %apply.1 = (f32[64,256]{1,0:T(8,128)}, f32[64,256]{1,0:T(8,128)}, f32[104,128]{1,0:T(8,128)S(1)}, f32[104,128]{1,0:T(8,128)S(1)}) custom-call(s32[1]{0:T(128)} %bitcast.me_ref, f32[16,40,128]{2,1,0:T(8,128)S(1)} %all_to_all.5.own_ref, f32[16,40,128]{2,1,0:T(8,128)S(1)} %collective-permute-done.other_ref, f32[16,72,128]{2,1,0:T(8,128)S(1)} %get-tuple-element.22.aug_ref, ...), custom_call_target="tpu_custom_call" | custom-call | tf_op jit(solution)/shard_map/apply/pallas_call | solution.py:539
  34.0 0.5 collective-permute-start.1
  34.5 0.9 %collective-permute-done.1 = f32[104,128]{1,0:T(8,128)S(1)} collective-permute-done((f32[104,128]{1,0:T(8,128)S(1)}, f32[104,128]{1,0:T(8,128)S(1)}, u32[]{:S(2)}, u32[]{:S(2)}) %collective-permute-start.1) | collective-permute-done | bytes 53280 | tf_op jit(solution)/shard_map/ppermute | solution.py:486
  35.4 3.8 %collective-permute-start.4 = (f32[104,128]{1,0:T(8,128)S(1)}, f32[104,128]{1,0:T(8,128)S(1)}, u32[]{:S(2)}, u32[]{:S(2)}) collective-permute-start(f32[104,128]{1,0:T(8,128)S(1)} %add.30), channel_id=1, source_target_pairs={{0,96},{32,64},{64,32},{96,0},{1,97},{33,65},{65,33},{97,1},{2,98}... | collective-permute-start | bytes 159752 | tf_op jit(solution)/shard_map/ppermute | solution.py:492
  39.2 0.0 collective-permute-start.3
  39.2 0.7 %collective-permute-start.2 = (f32[104,128]{1,0:T(8,128)S(1)}, f32[104,128]{1,0:T(8,128)S(1)}, u32[]{:S(2)}, u32[]{:S(2)}) collective-permute-start(f32[104,128]{1,0:T(8,128)S(1)} %add.30), channel_id=1, source_target_pairs={{0,32},{32,0},{64,96},{96,64},{1,33},{33,1},{65,97},{97,65},{2,34}... | collective-permute-start | bytes 159752 | tf_op jit(solution)/shard_map/ppermute | solution.py:492
  39.8 1.2 %collective-permute-done.4 = f32[104,128]{1,0:T(8,128)S(1)} collective-permute-done((f32[104,128]{1,0:T(8,128)S(1)}, f32[104,128]{1,0:T(8,128)S(1)}, u32[]{:S(2)}, u32[]{:S(2)}) %collective-permute-start.4) | collective-permute-done | bytes 53280 | tf_op jit(solution)/shard_map/ppermute | solution.py:492
  41.1 2.6 %collective-permute-done.3 = f32[104,128]{1,0:T(8,128)S(1)} collective-permute-done((f32[104,128]{1,0:T(8,128)S(1)}, f32[104,128]{1,0:T(8,128)S(1)}, u32[]{:S(2)}, u32[]{:S(2)}) %collective-permute-start.3) | collective-permute-done | bytes 53280 | tf_op jit(solution)/shard_map/ppermute | solution.py:492
  43.7 0.0 collective-permute-done.2
  43.7 0.7 %collective-permute-start.7 = (f32[104,128]{1,0:T(8,128)S(1)}, f32[104,128]{1,0:T(8,128)S(1)}, u32[]{:S(2)}, u32[]{:S(2)}) collective-permute-start(f32[104,128]{1,0:T(8,128)S(1)} %add_add_fusion.2), channel_id=1, source_target_pairs={{0,24},{1,25},{2,26},{3,27},{4,28},{5,29},{6,30},{7,31},{8,16},{9,... | collective-permute-start | bytes 159752 | tf_op jit(solution)/shard_map/ppermute | solution.py:492
  44.3 0.8 %collective-permute-start.6 = (f32[104,128]{1,0:T(8,128)S(1)}, f32[104,128]{1,0:T(8,128)S(1)}, u32[]{:S(2)}, u32[]{:S(2)}) collective-permute-start(f32[104,128]{1,0:T(8,128)S(1)} %add_add_fusion.2), channel_id=1, source_target_pairs={{0,16},{1,17},{2,18},{3,19},{4,20},{5,21},{6,22},{7,23},{8,24},{9,... | collective-permute-start | bytes 159752 | tf_op jit(solution)/shard_map/ppermute | solution.py:492
  45.2 1.8 %collective-permute-start.5 = (f32[104,128]{1,0:T(8,128)S(1)}, f32[104,128]{1,0:T(8,128)S(1)}, u32[]{:S(2)}, u32[]{:S(2)}) collective-permute-start(f32[104,128]{1,0:T(8,128)S(1)} %add_add_fusion.2), channel_id=1, source_target_pairs={{0,8},{1,9},{2,10},{3,11},{4,12},{5,13},{6,14},{7,15},{8,0},{9,1},... | collective-permute-start | bytes 159752 | tf_op jit(solution)/shard_map/ppermute | solution.py:492
  47.0 0.9 %collective-permute-done.7 = f32[104,128]{1,0:T(8,128)S(1)} collective-permute-done((f32[104,128]{1,0:T(8,128)S(1)}, f32[104,128]{1,0:T(8,128)S(1)}, u32[]{:S(2)}, u32[]{:S(2)}) %collective-permute-start.7) | collective-permute-done | bytes 53280 | tf_op jit(solution)/shard_map/ppermute | solution.py:492
  48.0 0.9 %collective-permute-done.6 = f32[104,128]{1,0:T(8,128)S(1)} collective-permute-done((f32[104,128]{1,0:T(8,128)S(1)}, f32[104,128]{1,0:T(8,128)S(1)}, u32[]{:S(2)}, u32[]{:S(2)}) %collective-permute-start.6) | collective-permute-done | bytes 53280 | tf_op jit(solution)/shard_map/ppermute | solution.py:492
  48.8 0.3 collective-permute-done.5
  49.1 0.4 collective-permute-start.10
  49.5 1.7 %collective-permute-start.9 = (f32[104,128]{1,0:T(8,128)S(1)}, f32[104,128]{1,0:T(8,128)S(1)}, u32[]{:S(2)}, u32[]{:S(2)}) collective-permute-start(f32[104,128]{1,0:T(8,128)S(1)} %add_add_fusion.1), channel_id=1, source_target_pairs={{0,4},{1,5},{2,6},{3,7},{4,0},{5,1},{6,2},{7,3},{8,12},{9,13},{10,... | collective-permute-start | bytes 159752 | tf_op jit(solution)/shard_map/ppermute | solution.py:492
  51.3 1.2 %collective-permute-start.8 = (f32[104,128]{1,0:T(8,128)S(1)}, f32[104,128]{1,0:T(8,128)S(1)}, u32[]{:S(2)}, u32[]{:S(2)}) collective-permute-start(f32[104,128]{1,0:T(8,128)S(1)} %add_add_fusion.1), channel_id=1, source_target_pairs={{0,2},{1,3},{2,0},{3,1},{4,6},{5,7},{6,4},{7,5},{8,10},{9,11},{10,... | collective-permute-start | bytes 159752 | tf_op jit(solution)/shard_map/ppermute | solution.py:492
  52.5 0.9 %collective-permute-done.10 = f32[104,128]{1,0:T(8,128)S(1)} collective-permute-done((f32[104,128]{1,0:T(8,128)S(1)}, f32[104,128]{1,0:T(8,128)S(1)}, u32[]{:S(2)}, u32[]{:S(2)}) %collective-permute-start.10) | collective-permute-done | bytes 53280 | tf_op jit(solution)/shard_map/ppermute | solution.py:492
  53.4 0.6 %collective-permute-done.9 = f32[104,128]{1,0:T(8,128)S(1)} collective-permute-done((f32[104,128]{1,0:T(8,128)S(1)}, f32[104,128]{1,0:T(8,128)S(1)}, u32[]{:S(2)}, u32[]{:S(2)}) %collective-permute-start.9) | collective-permute-done | bytes 53280 | tf_op jit(solution)/shard_map/ppermute | solution.py:492
  54.0 0.5 collective-permute-done.8
  54.6 4.8 %collective-permute-start.11 = (f32[104,128]{1,0:T(8,128)S(1)}, f32[104,128]{1,0:T(8,128)S(1)}, u32[]{:S(2)}, u32[]{:S(2)}) collective-permute-start(f32[104,128]{1,0:T(8,128)S(1)} %add_add_fusion.own_ref), channel_id=1, source_target_pairs={{0,1},{1,0},{2,3},{3,2},{4,5},{5,4},{6,7},{7,6},{8,9},{9,8},{10,11... | collective-permute-start | bytes 159752 | tf_op jit(solution)/shard_map/ppermute | solution.py:486
  59.3 0.9 %collective-permute-done.11.other_ref = f32[104,128]{1,0:T(8,128)S(1)} collective-permute-done((f32[104,128]{1,0:T(8,128)S(1)}, f32[104,128]{1,0:T(8,128)S(1)}, u32[]{:S(2)}, u32[]{:S(2)}) %collective-permute-start.11) | collective-permute-done | bytes 53280 | tf_op jit(solution)/shard_map/ppermute | solution.py:486
  60.2 0.7 %finish.1 = (f32[64,192]{1,0:T(8,128)}, f32[64,192]{1,0:T(8,128)}, f32[2,128]{1,0:T(2,128)}) custom-call(s32[1]{0:T(128)} %bitcast.me_ref, f32[104,128]{1,0:T(8,128)S(1)} %add_add_fusion.own_ref, f32[104,128]{1,0:T(8,128)S(1)} %collective-permute-done.11.other_ref), custom_call_target="tpu_custom_call" | custom-call | tf_op jit(solution)/shard_map/finish/pallas_call | solution.py:560
  (4 shorter events, 0.1 us)
Async XLA Ops:
  24.0 3.1 %collective-permute-start = (f32[16,40,128]{2,1,0:T(8,128)S(1)}, f32[16,40,128]{2,1,0:T(8,128)S(1)}, u32[]{:S(2)}, u32[]{:S(2)}) collective-permute-start(f32[16,40,128]{2,1,0:T(8,128)S(1)} %all_to_all.5.own_ref), channel_id=1, source_target_pairs={{0,1},{1,0},{2,3},{3,2},{4,5},{5,4},{6,7},{7,6},{8,9},{9,8},{10,11... | collective-permute-start | bytes 983048 | tf_op jit(solution)/shard_map/ppermute | solution.py:486
  34.0 1.3 %collective-permute-start.1 = (f32[104,128]{1,0:T(8,128)S(1)}, f32[104,128]{1,0:T(8,128)S(1)}, u32[]{:S(2)}, u32[]{:S(2)}) collective-permute-start(f32[104,128]{1,0:T(8,128)S(1)} %get-tuple-element.33), channel_id=1, source_target_pairs={{0,1},{1,0},{2,3},{3,2},{4,5},{5,4},{6,7},{7,6},{8,9},{9,8},{10,11... | collective-permute-start | bytes 159752 | tf_op jit(solution)/shard_map/ppermute | solution.py:486
  35.4 5.7 %collective-permute-start.4 = (f32[104,128]{1,0:T(8,128)S(1)}, f32[104,128]{1,0:T(8,128)S(1)}, u32[]{:S(2)}, u32[]{:S(2)}) collective-permute-start(f32[104,128]{1,0:T(8,128)S(1)} %add.30), channel_id=1, source_target_pairs={{0,96},{32,64},{64,32},{96,0},{1,97},{33,65},{65,33},{97,1},{2,98}... | collective-permute-start | bytes 159752 | tf_op jit(solution)/shard_map/ppermute | solution.py:492
  39.2 4.5 %collective-permute-start.3 = (f32[104,128]{1,0:T(8,128)S(1)}, f32[104,128]{1,0:T(8,128)S(1)}, u32[]{:S(2)}, u32[]{:S(2)}) collective-permute-start(f32[104,128]{1,0:T(8,128)S(1)} %add.30), channel_id=1, source_target_pairs={{0,64},{32,96},{64,0},{96,32},{1,65},{33,97},{65,1},{97,33},{2,66}... | collective-permute-start | bytes 159752 | tf_op jit(solution)/shard_map/ppermute | solution.py:492
  39.2 4.5 %collective-permute-start.2 = (f32[104,128]{1,0:T(8,128)S(1)}, f32[104,128]{1,0:T(8,128)S(1)}, u32[]{:S(2)}, u32[]{:S(2)}) collective-permute-start(f32[104,128]{1,0:T(8,128)S(1)} %add.30), channel_id=1, source_target_pairs={{0,32},{32,0},{64,96},{96,64},{1,33},{33,1},{65,97},{97,65},{2,34}... | collective-permute-start | bytes 159752 | tf_op jit(solution)/shard_map/ppermute | solution.py:492
  43.7 4.3 %collective-permute-start.7 = (f32[104,128]{1,0:T(8,128)S(1)}, f32[104,128]{1,0:T(8,128)S(1)}, u32[]{:S(2)}, u32[]{:S(2)}) collective-permute-start(f32[104,128]{1,0:T(8,128)S(1)} %add_add_fusion.2), channel_id=1, source_target_pairs={{0,24},{1,25},{2,26},{3,27},{4,28},{5,29},{6,30},{7,31},{8,16},{9,... | collective-permute-start | bytes 159752 | tf_op jit(solution)/shard_map/ppermute | solution.py:492
  44.3 4.5 %collective-permute-start.6 = (f32[104,128]{1,0:T(8,128)S(1)}, f32[104,128]{1,0:T(8,128)S(1)}, u32[]{:S(2)}, u32[]{:S(2)}) collective-permute-start(f32[104,128]{1,0:T(8,128)S(1)} %add_add_fusion.2), channel_id=1, source_target_pairs={{0,16},{1,17},{2,18},{3,19},{4,20},{5,21},{6,22},{7,23},{8,24},{9,... | collective-permute-start | bytes 159752 | tf_op jit(solution)/shard_map/ppermute | solution.py:492
  45.2 3.9 %collective-permute-start.5 = (f32[104,128]{1,0:T(8,128)S(1)}, f32[104,128]{1,0:T(8,128)S(1)}, u32[]{:S(2)}, u32[]{:S(2)}) collective-permute-start(f32[104,128]{1,0:T(8,128)S(1)} %add_add_fusion.2), channel_id=1, source_target_pairs={{0,8},{1,9},{2,10},{3,11},{4,12},{5,13},{6,14},{7,15},{8,0},{9,1},... | collective-permute-start | bytes 159752 | tf_op jit(solution)/shard_map/ppermute | solution.py:492
  49.1 4.3 %collective-permute-start.10 = (f32[104,128]{1,0:T(8,128)S(1)}, f32[104,128]{1,0:T(8,128)S(1)}, u32[]{:S(2)}, u32[]{:S(2)}) collective-permute-start(f32[104,128]{1,0:T(8,128)S(1)} %add_add_fusion.1), channel_id=1, source_target_pairs={{0,6},{1,7},{2,4},{3,5},{4,2},{5,3},{6,0},{7,1},{8,14},{9,15},{10,... | collective-permute-start | bytes 159752 | tf_op jit(solution)/shard_map/ppermute | solution.py:492
  49.5 4.5 %collective-permute-start.9 = (f32[104,128]{1,0:T(8,128)S(1)}, f32[104,128]{1,0:T(8,128)S(1)}, u32[]{:S(2)}, u32[]{:S(2)}) collective-permute-start(f32[104,128]{1,0:T(8,128)S(1)} %add_add_fusion.1), channel_id=1, source_target_pairs={{0,4},{1,5},{2,6},{3,7},{4,0},{5,1},{6,2},{7,3},{8,12},{9,13},{10,... | collective-permute-start | bytes 159752 | tf_op jit(solution)/shard_map/ppermute | solution.py:492
  51.3 3.3 %collective-permute-start.8 = (f32[104,128]{1,0:T(8,128)S(1)}, f32[104,128]{1,0:T(8,128)S(1)}, u32[]{:S(2)}, u32[]{:S(2)}) collective-permute-start(f32[104,128]{1,0:T(8,128)S(1)} %add_add_fusion.1), channel_id=1, source_target_pairs={{0,2},{1,3},{2,0},{3,1},{4,6},{5,7},{6,4},{7,5},{8,10},{9,11},{10,... | collective-permute-start | bytes 159752 | tf_op jit(solution)/shard_map/ppermute | solution.py:492
  54.6 5.7 %collective-permute-start.11 = (f32[104,128]{1,0:T(8,128)S(1)}, f32[104,128]{1,0:T(8,128)S(1)}, u32[]{:S(2)}, u32[]{:S(2)}) collective-permute-start(f32[104,128]{1,0:T(8,128)S(1)} %add_add_fusion.own_ref), channel_id=1, source_target_pairs={{0,1},{1,0},{2,3},{3,2},{4,5},{5,4},{6,7},{7,6},{8,9},{9,8},{10,11... | collective-permute-start | bytes 159752 | tf_op jit(solution)/shard_map/ppermute | solution.py:486

commit v7 on v6

--- a/solution.py
+++ b/solution.py
@@ -488,10 +488,10 @@
 
 def summed_by_four(a, axis, stride):
     count = lax.axis_size(axis)
-    one, two, three_off = [
+    first, second, third = [
         lax.ppermute(a, axis, [(k, k ^ (step * stride)) for k in range(count)]) for step in (1, 2, 3)
     ]
-    return lax.optimization_barrier((a + one) + (two + three_off))
+    return lax.optimization_barrier((first + third) + (a + second))
 
 
 def per_device(inputs, guess, cotangent, w_input, w_hidden, bias):

time: 61.2 us -> 60.9 us (level)
  starting transfers between devices: 18.2 us -> 17.1 us
  waiting for transfers between devices: 11 us -> 11.9 us
    ppermute x9, starting transfers between devices: 11.2 us -> 9.86 us  [summed_by_four(): lax.ppermute(a, axis, [(k, k ^ step * stride) for k in range(count)])]
    ppermute x9, waiting for transfers between devices: 7.99 us -> 8.9 us  [summed_by_four(): lax.ppermute(a, axis, [(k, k ^ step * stride) for k in range(count)])]
where the time goes in v7:
time: 60.9 us; the launch traced here: 60.7 us
  starting transfers between devices  17.1 us (28%)
  blocking collectives  15.9 us (26%)
  Pallas kernels  15.1 us (25%)
  waiting for transfers between devices  11.9 us (20%)
  between operations  0.66 us (1%)
    all_to_all x1, blocking collectives, per_device(): received = lax.all_to_all(send, 'tm', 0, 0, axis_index_groups=groups)  15.9 us
    ppermute x9, starting transfers between devices, summed_by_four(): lax.ppermute(a, axis, [(k, k ^ step * stride) for k in range(count)])  9.86 us
    ppermute x9, waiting for transfers between devices, summed_by_four(): lax.ppermute(a, axis, [(k, k ^ step * stride) for k in range(count)])  8.9 us
    pallas_call x1, Pallas kernels, per_device(): pl.pallas_call(blocks_kernel, out_shape=(shape(HALF, TILE, 128), shape(16...  7.55 us
    ppermute x3, starting transfers between devices, swapped(): return lax.ppermute(a, 'tm', [(k, k ^ 1) for k in range(DEV)])  7.25 us
    pallas_call x1, Pallas kernels, per_device(): pl.pallas_call(apply_kernel, out_shape=(shape(H, T), shape(H, T), shape(P...  6.83 us
    ppermute x3, waiting for transfers between devices, swapped(): return lax.ppermute(a, 'tm', [(k, k ^ 1) for k in range(DEV)])  3.03 us
  transfers between devices with their start and end apart: 12, of which 11 were waited for; matrix products, arithmetic and copies ran while one was open for 0% of the time, Pallas kernels for 0%

profile of v7, /device:TPU:1, one launch (start us, length us, event | category | flops | bytes accessed | tf_op | source)
XLA Modules:
  0.0 60.7 jit_solution(12616792225387814847)
XLA Ops:
  0.6 7.5 %blocks.1 = (f32[16,40,128]{2,1,0:T(8,128)S(1)}, f32[16,72,128]{2,1,0:T(8,128)S(1)}, f32[4,72,128]{2,1,0:T(8,128)S(1)}, f32[6,128,128]{2,1,0:T(8,128)S(1)}, f32[...) custom-call(f32[64,256]{1,0:T(8,128)} %bitcast.18, ...), custom_call_target="tpu_custom_call" | custom-call | tf_op jit(solution)/shard_map/blocks/pallas_call | solution.py:511
  8.2 15.9 %all_to_all.5.own_ref = f32[16,40,128]{2,1,0:T(8,128)S(1)} all-to-all(f32[16,40,128]{2,1,0:T(8,128)S(1)} %get-tuple-element.21), channel_id=1, replica_groups={{0,2,4,6,8,10,12,14,16,18,20,22,24,26,28,30},{1,3,5,7,9,11,13,15,17,19,..., dimensions={0} | all-to-all | bytes 655360 | tf_op jit(solution)/shard_map/all_to_all | solution.py:536
  24.0 1.9 %collective-permute-start = (f32[16,40,128]{2,1,0:T(8,128)S(1)}, f32[16,40,128]{2,1,0:T(8,128)S(1)}, u32[]{:S(2)}, u32[]{:S(2)}) collective-permute-start(f32[16,40,128]{2,1,0:T(8,128)S(1)} %all_to_all.5.own_ref), channel_id=1, source_target_pairs={{0,1},{1,0},{2,3},{3,2},{4,5},{5,4},{6,7},{7,6},{8,9},{9,8},{10,11... | collective-permute-start | bytes 983048 | tf_op jit(solution)/shard_map/ppermute | solution.py:486
  25.9 1.3 %collective-permute-done.other_ref = f32[16,40,128]{2,1,0:T(8,128)S(1)} collective-permute-done((f32[16,40,128]{2,1,0:T(8,128)S(1)}, f32[16,40,128]{2,1,0:T(8,128)S(1)}, u32[]{:S(2)}, u32[]{:S(2)}) %collective-permute-start) | collective-permute-done | bytes 327712 | tf_op jit(solution)/shard_map/ppermute | solution.py:486
  27.2 6.8 %apply.1 = (f32[64,256]{1,0:T(8,128)}, f32[64,256]{1,0:T(8,128)}, f32[104,128]{1,0:T(8,128)S(1)}, f32[104,128]{1,0:T(8,128)S(1)}) custom-call(s32[1]{0:T(128)} %bitcast.me_ref, f32[16,40,128]{2,1,0:T(8,128)S(1)} %all_to_all.5.own_ref, f32[16,40,128]{2,1,0:T(8,128)S(1)} %collective-permute-done.other_ref, f32[16,72,128]{2,1,0:T(8,128)S(1)} %get-tuple-element.22.aug_ref, ...), custom_call_target="tpu_custom_call" | custom-call | tf_op jit(solution)/shard_map/apply/pallas_call | solution.py:539
  34.0 0.5 collective-permute-start.1
  34.5 0.9 %collective-permute-done.1 = f32[104,128]{1,0:T(8,128)S(1)} collective-permute-done((f32[104,128]{1,0:T(8,128)S(1)}, f32[104,128]{1,0:T(8,128)S(1)}, u32[]{:S(2)}, u32[]{:S(2)}) %collective-permute-start.1) | collective-permute-done | bytes 53280 | tf_op jit(solution)/shard_map/ppermute | solution.py:486
  35.4 3.7 %collective-permute-start.4 = (f32[104,128]{1,0:T(8,128)S(1)}, f32[104,128]{1,0:T(8,128)S(1)}, u32[]{:S(2)}, u32[]{:S(2)}) collective-permute-start(f32[104,128]{1,0:T(8,128)S(1)} %add.30), channel_id=1, source_target_pairs={{0,64},{32,96},{64,0},{96,32},{1,65},{33,97},{65,1},{97,33},{2,66}... | collective-permute-start | bytes 159752 | tf_op jit(solution)/shard_map/ppermute | solution.py:492
  39.0 0.4 collective-permute-start.3
  39.4 0.3 collective-permute-start.2
  39.8 1.2 %collective-permute-done.4 = f32[104,128]{1,0:T(8,128)S(1)} collective-permute-done((f32[104,128]{1,0:T(8,128)S(1)}, f32[104,128]{1,0:T(8,128)S(1)}, u32[]{:S(2)}, u32[]{:S(2)}) %collective-permute-start.4) | collective-permute-done | bytes 53280 | tf_op jit(solution)/shard_map/ppermute | solution.py:492
  40.9 2.3 %collective-permute-done.3 = f32[104,128]{1,0:T(8,128)S(1)} collective-permute-done((f32[104,128]{1,0:T(8,128)S(1)}, f32[104,128]{1,0:T(8,128)S(1)}, u32[]{:S(2)}, u32[]{:S(2)}) %collective-permute-start.3) | collective-permute-done | bytes 53280 | tf_op jit(solution)/shard_map/ppermute | solution.py:492
  43.2 0.0 collective-permute-done.2
  43.2 0.7 %collective-permute-start.7 = (f32[104,128]{1,0:T(8,128)S(1)}, f32[104,128]{1,0:T(8,128)S(1)}, u32[]{:S(2)}, u32[]{:S(2)}) collective-permute-start(f32[104,128]{1,0:T(8,128)S(1)} %add_add_fusion.2), channel_id=1, source_target_pairs={{0,16},{1,17},{2,18},{3,19},{4,20},{5,21},{6,22},{7,23},{8,24},{9,... | collective-permute-start | bytes 159752 | tf_op jit(solution)/shard_map/ppermute | solution.py:492
  43.9 1.4 %collective-permute-start.6 = (f32[104,128]{1,0:T(8,128)S(1)}, f32[104,128]{1,0:T(8,128)S(1)}, u32[]{:S(2)}, u32[]{:S(2)}) collective-permute-start(f32[104,128]{1,0:T(8,128)S(1)} %add_add_fusion.2), channel_id=1, source_target_pairs={{0,24},{1,25},{2,26},{3,27},{4,28},{5,29},{6,30},{7,31},{8,16},{9,... | collective-permute-start | bytes 159752 | tf_op jit(solution)/shard_map/ppermute | solution.py:492
  45.3 0.6 %collective-permute-start.5 = (f32[104,128]{1,0:T(8,128)S(1)}, f32[104,128]{1,0:T(8,128)S(1)}, u32[]{:S(2)}, u32[]{:S(2)}) collective-permute-start(f32[104,128]{1,0:T(8,128)S(1)} %add_add_fusion.2), channel_id=1, source_target_pairs={{0,8},{1,9},{2,10},{3,11},{4,12},{5,13},{6,14},{7,15},{8,0},{9,1},... | collective-permute-start | bytes 159752 | tf_op jit(solution)/shard_map/ppermute | solution.py:492
  46.0 1.9 %collective-permute-done.7 = f32[104,128]{1,0:T(8,128)S(1)} collective-permute-done((f32[104,128]{1,0:T(8,128)S(1)}, f32[104,128]{1,0:T(8,128)S(1)}, u32[]{:S(2)}, u32[]{:S(2)}) %collective-permute-start.7) | collective-permute-done | bytes 53280 | tf_op jit(solution)/shard_map/ppermute | solution.py:492
  47.8 0.5 collective-permute-done.6
  48.4 0.4 collective-permute-done.5
  48.8 1.0 %collective-permute-start.10 = (f32[104,128]{1,0:T(8,128)S(1)}, f32[104,128]{1,0:T(8,128)S(1)}, u32[]{:S(2)}, u32[]{:S(2)}) collective-permute-start(f32[104,128]{1,0:T(8,128)S(1)} %add_add_fusion.1), channel_id=1, source_target_pairs={{0,4},{1,5},{2,6},{3,7},{4,0},{5,1},{6,2},{7,3},{8,12},{9,13},{10,... | collective-permute-start | bytes 159752 | tf_op jit(solution)/shard_map/ppermute | solution.py:492
  49.8 1.4 %collective-permute-start.9 = (f32[104,128]{1,0:T(8,128)S(1)}, f32[104,128]{1,0:T(8,128)S(1)}, u32[]{:S(2)}, u32[]{:S(2)}) collective-permute-start(f32[104,128]{1,0:T(8,128)S(1)} %add_add_fusion.1), channel_id=1, source_target_pairs={{0,6},{1,7},{2,4},{3,5},{4,2},{5,3},{6,0},{7,1},{8,14},{9,15},{10,... | collective-permute-start | bytes 159752 | tf_op jit(solution)/shard_map/ppermute | solution.py:492
  51.2 0.4 collective-permute-start.8
  51.6 1.8 %collective-permute-done.10 = f32[104,128]{1,0:T(8,128)S(1)} collective-permute-done((f32[104,128]{1,0:T(8,128)S(1)}, f32[104,128]{1,0:T(8,128)S(1)}, u32[]{:S(2)}, u32[]{:S(2)}) %collective-permute-start.10) | collective-permute-done | bytes 53280 | tf_op jit(solution)/shard_map/ppermute | solution.py:492
  53.4 0.6 collective-permute-done.9
  54.0 0.2 collective-permute-done.8
  54.2 4.9 %collective-permute-start.11 = (f32[104,128]{1,0:T(8,128)S(1)}, f32[104,128]{1,0:T(8,128)S(1)}, u32[]{:S(2)}, u32[]{:S(2)}) collective-permute-start(f32[104,128]{1,0:T(8,128)S(1)} %add_add_fusion.own_ref), channel_id=1, source_target_pairs={{0,1},{1,0},{2,3},{3,2},{4,5},{5,4},{6,7},{7,6},{8,9},{9,8},{10,11... | collective-permute-start | bytes 159752 | tf_op jit(solution)/shard_map/ppermute | solution.py:486
  59.1 0.9 %collective-permute-done.11.other_ref = f32[104,128]{1,0:T(8,128)S(1)} collective-permute-done((f32[104,128]{1,0:T(8,128)S(1)}, f32[104,128]{1,0:T(8,128)S(1)}, u32[]{:S(2)}, u32[]{:S(2)}) %collective-permute-start.11) | collective-permute-done | bytes 53280 | tf_op jit(solution)/shard_map/ppermute | solution.py:486
  60.0 0.7 %finish.1 = (f32[64,192]{1,0:T(8,128)}, f32[64,192]{1,0:T(8,128)}, f32[2,128]{1,0:T(2,128)}) custom-call(s32[1]{0:T(128)} %bitcast.me_ref, f32[104,128]{1,0:T(8,128)S(1)} %add_add_fusion.own_ref, f32[104,128]{1,0:T(8,128)S(1)} %collective-permute-done.11.other_ref), custom_call_target="tpu_custom_call" | custom-call | tf_op jit(solution)/shard_map/finish/pallas_call | solution.py:560
  (4 shorter events, 0.1 us)
Async XLA Ops:
  24.0 3.1 %collective-permute-start = (f32[16,40,128]{2,1,0:T(8,128)S(1)}, f32[16,40,128]{2,1,0:T(8,128)S(1)}, u32[]{:S(2)}, u32[]{:S(2)}) collective-permute-start(f32[16,40,128]{2,1,0:T(8,128)S(1)} %all_to_all.5.own_ref), channel_id=1, source_target_pairs={{0,1},{1,0},{2,3},{3,2},{4,5},{5,4},{6,7},{7,6},{8,9},{9,8},{10,11... | collective-permute-start | bytes 983048 | tf_op jit(solution)/shard_map/ppermute | solution.py:486
  34.0 1.3 %collective-permute-start.1 = (f32[104,128]{1,0:T(8,128)S(1)}, f32[104,128]{1,0:T(8,128)S(1)}, u32[]{:S(2)}, u32[]{:S(2)}) collective-permute-start(f32[104,128]{1,0:T(8,128)S(1)} %get-tuple-element.33), channel_id=1, source_target_pairs={{0,1},{1,0},{2,3},{3,2},{4,5},{5,4},{6,7},{7,6},{8,9},{9,8},{10,11... | collective-permute-start | bytes 159752 | tf_op jit(solution)/shard_map/ppermute | solution.py:486
  35.4 5.6 %collective-permute-start.4 = (f32[104,128]{1,0:T(8,128)S(1)}, f32[104,128]{1,0:T(8,128)S(1)}, u32[]{:S(2)}, u32[]{:S(2)}) collective-permute-start(f32[104,128]{1,0:T(8,128)S(1)} %add.30), channel_id=1, source_target_pairs={{0,64},{32,96},{64,0},{96,32},{1,65},{33,97},{65,1},{97,33},{2,66}... | collective-permute-start | bytes 159752 | tf_op jit(solution)/shard_map/ppermute | solution.py:492
  39.0 4.2 %collective-permute-start.3 = (f32[104,128]{1,0:T(8,128)S(1)}, f32[104,128]{1,0:T(8,128)S(1)}, u32[]{:S(2)}, u32[]{:S(2)}) collective-permute-start(f32[104,128]{1,0:T(8,128)S(1)} %add.30), channel_id=1, source_target_pairs={{0,96},{32,64},{64,32},{96,0},{1,97},{33,65},{65,33},{97,1},{2,98}... | collective-permute-start | bytes 159752 | tf_op jit(solution)/shard_map/ppermute | solution.py:492
  39.4 3.8 %collective-permute-start.2 = (f32[104,128]{1,0:T(8,128)S(1)}, f32[104,128]{1,0:T(8,128)S(1)}, u32[]{:S(2)}, u32[]{:S(2)}) collective-permute-start(f32[104,128]{1,0:T(8,128)S(1)} %add.30), channel_id=1, source_target_pairs={{0,32},{32,0},{64,96},{96,64},{1,33},{33,1},{65,97},{97,65},{2,34}... | collective-permute-start | bytes 159752 | tf_op jit(solution)/shard_map/ppermute | solution.py:492
  43.2 4.6 %collective-permute-start.7 = (f32[104,128]{1,0:T(8,128)S(1)}, f32[104,128]{1,0:T(8,128)S(1)}, u32[]{:S(2)}, u32[]{:S(2)}) collective-permute-start(f32[104,128]{1,0:T(8,128)S(1)} %add_add_fusion.2), channel_id=1, source_target_pairs={{0,16},{1,17},{2,18},{3,19},{4,20},{5,21},{6,22},{7,23},{8,24},{9,... | collective-permute-start | bytes 159752 | tf_op jit(solution)/shard_map/ppermute | solution.py:492
  43.9 4.5 %collective-permute-start.6 = (f32[104,128]{1,0:T(8,128)S(1)}, f32[104,128]{1,0:T(8,128)S(1)}, u32[]{:S(2)}, u32[]{:S(2)}) collective-permute-start(f32[104,128]{1,0:T(8,128)S(1)} %add_add_fusion.2), channel_id=1, source_target_pairs={{0,24},{1,25},{2,26},{3,27},{4,28},{5,29},{6,30},{7,31},{8,16},{9,... | collective-permute-start | bytes 159752 | tf_op jit(solution)/shard_map/ppermute | solution.py:492
  45.3 3.5 %collective-permute-start.5 = (f32[104,128]{1,0:T(8,128)S(1)}, f32[104,128]{1,0:T(8,128)S(1)}, u32[]{:S(2)}, u32[]{:S(2)}) collective-permute-start(f32[104,128]{1,0:T(8,128)S(1)} %add_add_fusion.2), channel_id=1, source_target_pairs={{0,8},{1,9},{2,10},{3,11},{4,12},{5,13},{6,14},{7,15},{8,0},{9,1},... | collective-permute-start | bytes 159752 | tf_op jit(solution)/shard_map/ppermute | solution.py:492
  48.8 4.6 %collective-permute-start.10 = (f32[104,128]{1,0:T(8,128)S(1)}, f32[104,128]{1,0:T(8,128)S(1)}, u32[]{:S(2)}, u32[]{:S(2)}) collective-permute-start(f32[104,128]{1,0:T(8,128)S(1)} %add_add_fusion.1), channel_id=1, source_target_pairs={{0,4},{1,5},{2,6},{3,7},{4,0},{5,1},{6,2},{7,3},{8,12},{9,13},{10,... | collective-permute-start | bytes 159752 | tf_op jit(solution)/shard_map/ppermute | solution.py:492
  49.8 4.2 %collective-permute-start.9 = (f32[104,128]{1,0:T(8,128)S(1)}, f32[104,128]{1,0:T(8,128)S(1)}, u32[]{:S(2)}, u32[]{:S(2)}) collective-permute-start(f32[104,128]{1,0:T(8,128)S(1)} %add_add_fusion.1), channel_id=1, source_target_pairs={{0,6},{1,7},{2,4},{3,5},{4,2},{5,3},{6,0},{7,1},{8,14},{9,15},{10,... | collective-permute-start | bytes 159752 | tf_op jit(solution)/shard_map/ppermute | solution.py:492
  51.2 3.0 %collective-permute-start.8 = (f32[104,128]{1,0:T(8,128)S(1)}, f32[104,128]{1,0:T(8,128)S(1)}, u32[]{:S(2)}, u32[]{:S(2)}) collective-permute-start(f32[104,128]{1,0:T(8,128)S(1)} %add_add_fusion.1), channel_id=1, source_target_pairs={{0,2},{1,3},{2,0},{3,1},{4,6},{5,7},{6,4},{7,5},{8,10},{9,11},{10,... | collective-permute-start | bytes 159752 | tf_op jit(solution)/shard_map/ppermute | solution.py:492
  54.2 5.8 %collective-permute-start.11 = (f32[104,128]{1,0:T(8,128)S(1)}, f32[104,128]{1,0:T(8,128)S(1)}, u32[]{:S(2)}, u32[]{:S(2)}) collective-permute-start(f32[104,128]{1,0:T(8,128)S(1)} %add_add_fusion.own_ref), channel_id=1, source_target_pairs={{0,1},{1,0},{2,3},{3,2},{4,5},{5,4},{6,7},{7,6},{8,9},{9,8},{10,11... | collective-permute-start | bytes 159752 | tf_op jit(solution)/shard_map/ppermute | solution.py:486

commit v8 on v7

--- a/solution.py
+++ b/solution.py
@@ -29,6 +29,13 @@
 
 def bdot(a, b):
     return jnp.dot(a, b, preferred_element_type=F32)
+
+
+def gate_dot(weights, columns):
+    tall = stacked(weights.T)
+    wide = jnp.concatenate(split(columns), axis=1)
+    out = bdot(tall, wide)
+    return out[:192, :T] + out[192:, :T] + out[:192, T:]
 
 
 def iota(shape, axis):
@@ -156,8 +163,8 @@
     hb_ref[...] = jnp.where(iota((8, 128), 1) < H, pltpu.roll(hb, H, 1), hb)
     guess = g_ref[...]
     prev = pltpu.roll(guess, 1, 1)
-    gi = dot(wi_ref[...], x_ref[...], ((0,), (0,)))
-    gh = dot(wh, prev, ((0,), (0,)))
+    gi = gate_dot(wi_ref[...], x_ref[...])
+    gh = gate_dot(wh, prev)
     bias0 = jnp.broadcast_to(bias_ref[0:1, :], (128, 128)).T
     bias1 = jnp.broadcast_to(bias_ref[1:2, :], (128, 128)).T
     bias0 = jnp.concatenate([bias0, bias0], axis=1)

time: 60.9 us -> 60.8 us (level)
  no operation moved by 1% of the time
where the time goes in v8:
time: 60.8 us; the launch traced here: 60.6 us
  starting transfers between devices  17.1 us (28%)
  blocking collectives  15.9 us (26%)
  Pallas kernels  14.9 us (25%)
  waiting for transfers between devices  11.9 us (20%)
  between operations  0.66 us (1%)
    all_to_all x1, blocking collectives, per_device(): received = lax.all_to_all(send, 'tm', 0, 0, axis_index_groups=groups)  15.9 us
    ppermute x9, starting transfers between devices, summed_by_four(): lax.ppermute(a, axis, [(k, k ^ step * stride) for k in range(count)])  9.84 us
    ppermute x9, waiting for transfers between devices, summed_by_four(): lax.ppermute(a, axis, [(k, k ^ step * stride) for k in range(count)])  8.92 us
    pallas_call x1, Pallas kernels, per_device(): pl.pallas_call(blocks_kernel, out_shape=(shape(HALF, TILE, 128), shape(16...  7.38 us
    ppermute x3, starting transfers between devices, swapped(): return lax.ppermute(a, 'tm', [(k, k ^ 1) for k in range(DEV)])  7.26 us
    pallas_call x1, Pallas kernels, per_device(): pl.pallas_call(apply_kernel, out_shape=(shape(H, T), shape(H, T), shape(P...  6.83 us
    ppermute x3, waiting for transfers between devices, swapped(): return lax.ppermute(a, 'tm', [(k, k ^ 1) for k in range(DEV)])  3.03 us
  transfers between devices with their start and end apart: 12, of which 11 were waited for; matrix products, arithmetic and copies ran while one was open for 0% of the time, Pallas kernels for 0%

profile of v8, /device:TPU:1, one launch (start us, length us, event | category | flops | bytes accessed | tf_op | source)
XLA Modules:
  0.0 60.6 jit_solution(16738611858666491077)
XLA Ops:
  0.6 7.4 %blocks.1 = (f32[16,40,128]{2,1,0:T(8,128)S(1)}, f32[16,72,128]{2,1,0:T(8,128)S(1)}, f32[4,72,128]{2,1,0:T(8,128)S(1)}, f32[6,128,128]{2,1,0:T(8,128)S(1)}, f32[...) custom-call(f32[64,256]{1,0:T(8,128)} %bitcast.18, ...), custom_call_target="tpu_custom_call" | custom-call | tf_op jit(solution)/shard_map/blocks/pallas_call | solution.py:518
  8.0 15.9 %all_to_all.5.own_ref = f32[16,40,128]{2,1,0:T(8,128)S(1)} all-to-all(f32[16,40,128]{2,1,0:T(8,128)S(1)} %get-tuple-element.21), channel_id=1, replica_groups={{0,2,4,6,8,10,12,14,16,18,20,22,24,26,28,30},{1,3,5,7,9,11,13,15,17,19,..., dimensions={0} | all-to-all | bytes 655360 | tf_op jit(solution)/shard_map/all_to_all | solution.py:543
  23.9 1.9 %collective-permute-start = (f32[16,40,128]{2,1,0:T(8,128)S(1)}, f32[16,40,128]{2,1,0:T(8,128)S(1)}, u32[]{:S(2)}, u32[]{:S(2)}) collective-permute-start(f32[16,40,128]{2,1,0:T(8,128)S(1)} %all_to_all.5.own_ref), channel_id=1, source_target_pairs={{0,1},{1,0},{2,3},{3,2},{4,5},{5,4},{6,7},{7,6},{8,9},{9,8},{10,11... | collective-permute-start | bytes 983048 | tf_op jit(solution)/shard_map/ppermute | solution.py:493
  25.8 1.3 %collective-permute-done.other_ref = f32[16,40,128]{2,1,0:T(8,128)S(1)} collective-permute-done((f32[16,40,128]{2,1,0:T(8,128)S(1)}, f32[16,40,128]{2,1,0:T(8,128)S(1)}, u32[]{:S(2)}, u32[]{:S(2)}) %collective-permute-start) | collective-permute-done | bytes 327712 | tf_op jit(solution)/shard_map/ppermute | solution.py:493
  27.0 6.8 %apply.1 = (f32[64,256]{1,0:T(8,128)}, f32[64,256]{1,0:T(8,128)}, f32[104,128]{1,0:T(8,128)S(1)}, f32[104,128]{1,0:T(8,128)S(1)}) custom-call(s32[1]{0:T(128)} %bitcast.me_ref, f32[16,40,128]{2,1,0:T(8,128)S(1)} %all_to_all.5.own_ref, f32[16,40,128]{2,1,0:T(8,128)S(1)} %collective-permute-done.other_ref, f32[16,72,128]{2,1,0:T(8,128)S(1)} %get-tuple-element.22.aug_ref, ...), custom_call_target="tpu_custom_call" | custom-call | tf_op jit(solution)/shard_map/apply/pallas_call | solution.py:546
  33.9 0.5 collective-permute-start.1
  34.3 0.9 %collective-permute-done.1 = f32[104,128]{1,0:T(8,128)S(1)} collective-permute-done((f32[104,128]{1,0:T(8,128)S(1)}, f32[104,128]{1,0:T(8,128)S(1)}, u32[]{:S(2)}, u32[]{:S(2)}) %collective-permute-start.1) | collective-permute-done | bytes 53280 | tf_op jit(solution)/shard_map/ppermute | solution.py:493
  35.2 3.7 %collective-permute-start.4 = (f32[104,128]{1,0:T(8,128)S(1)}, f32[104,128]{1,0:T(8,128)S(1)}, u32[]{:S(2)}, u32[]{:S(2)}) collective-permute-start(f32[104,128]{1,0:T(8,128)S(1)} %add.30), channel_id=1, source_target_pairs={{0,64},{32,96},{64,0},{96,32},{1,65},{33,97},{65,1},{97,33},{2,66}... | collective-permute-start | bytes 159752 | tf_op jit(solution)/shard_map/ppermute | solution.py:499
  38.9 0.4 collective-permute-start.3
  39.3 0.3 collective-permute-start.2
  39.6 1.2 %collective-permute-done.4 = f32[104,128]{1,0:T(8,128)S(1)} collective-permute-done((f32[104,128]{1,0:T(8,128)S(1)}, f32[104,128]{1,0:T(8,128)S(1)}, u32[]{:S(2)}, u32[]{:S(2)}) %collective-permute-start.4) | collective-permute-done | bytes 53280 | tf_op jit(solution)/shard_map/ppermute | solution.py:499
  40.8 2.3 %collective-permute-done.3 = f32[104,128]{1,0:T(8,128)S(1)} collective-permute-done((f32[104,128]{1,0:T(8,128)S(1)}, f32[104,128]{1,0:T(8,128)S(1)}, u32[]{:S(2)}, u32[]{:S(2)}) %collective-permute-start.3) | collective-permute-done | bytes 53280 | tf_op jit(solution)/shard_map/ppermute | solution.py:499
  43.1 0.0 collective-permute-done.2
  43.1 0.7 %collective-permute-start.7 = (f32[104,128]{1,0:T(8,128)S(1)}, f32[104,128]{1,0:T(8,128)S(1)}, u32[]{:S(2)}, u32[]{:S(2)}) collective-permute-start(f32[104,128]{1,0:T(8,128)S(1)} %add_add_fusion.2), channel_id=1, source_target_pairs={{0,16},{1,17},{2,18},{3,19},{4,20},{5,21},{6,22},{7,23},{8,24},{9,... | collective-permute-start | bytes 159752 | tf_op jit(solution)/shard_map/ppermute | solution.py:499
  43.7 1.4 %collective-permute-start.6 = (f32[104,128]{1,0:T(8,128)S(1)}, f32[104,128]{1,0:T(8,128)S(1)}, u32[]{:S(2)}, u32[]{:S(2)}) collective-permute-start(f32[104,128]{1,0:T(8,128)S(1)} %add_add_fusion.2), channel_id=1, source_target_pairs={{0,24},{1,25},{2,26},{3,27},{4,28},{5,29},{6,30},{7,31},{8,16},{9,... | collective-permute-start | bytes 159752 | tf_op jit(solution)/shard_map/ppermute | solution.py:499
  45.2 0.6 %collective-permute-start.5 = (f32[104,128]{1,0:T(8,128)S(1)}, f32[104,128]{1,0:T(8,128)S(1)}, u32[]{:S(2)}, u32[]{:S(2)}) collective-permute-start(f32[104,128]{1,0:T(8,128)S(1)} %add_add_fusion.2), channel_id=1, source_target_pairs={{0,8},{1,9},{2,10},{3,11},{4,12},{5,13},{6,14},{7,15},{8,0},{9,1},... | collective-permute-start | bytes 159752 | tf_op jit(solution)/shard_map/ppermute | solution.py:499
  45.8 1.9 %collective-permute-done.7 = f32[104,128]{1,0:T(8,128)S(1)} collective-permute-done((f32[104,128]{1,0:T(8,128)S(1)}, f32[104,128]{1,0:T(8,128)S(1)}, u32[]{:S(2)}, u32[]{:S(2)}) %collective-permute-start.7) | collective-permute-done | bytes 53280 | tf_op jit(solution)/shard_map/ppermute | solution.py:499
  47.7 0.5 collective-permute-done.6
  48.2 0.4 collective-permute-done.5
  48.7 1.0 %collective-permute-start.10 = (f32[104,128]{1,0:T(8,128)S(1)}, f32[104,128]{1,0:T(8,128)S(1)}, u32[]{:S(2)}, u32[]{:S(2)}) collective-permute-start(f32[104,128]{1,0:T(8,128)S(1)} %add_add_fusion.1), channel_id=1, source_target_pairs={{0,4},{1,5},{2,6},{3,7},{4,0},{5,1},{6,2},{7,3},{8,12},{9,13},{10,... | collective-permute-start | bytes 159752 | tf_op jit(solution)/shard_map/ppermute | solution.py:499
  49.6 1.4 %collective-permute-start.9 = (f32[104,128]{1,0:T(8,128)S(1)}, f32[104,128]{1,0:T(8,128)S(1)}, u32[]{:S(2)}, u32[]{:S(2)}) collective-permute-start(f32[104,128]{1,0:T(8,128)S(1)} %add_add_fusion.1), channel_id=1, source_target_pairs={{0,6},{1,7},{2,4},{3,5},{4,2},{5,3},{6,0},{7,1},{8,14},{9,15},{10,... | collective-permute-start | bytes 159752 | tf_op jit(solution)/shard_map/ppermute | solution.py:499
  51.0 0.4 collective-permute-start.8
  51.4 1.8 %collective-permute-done.10 = f32[104,128]{1,0:T(8,128)S(1)} collective-permute-done((f32[104,128]{1,0:T(8,128)S(1)}, f32[104,128]{1,0:T(8,128)S(1)}, u32[]{:S(2)}, u32[]{:S(2)}) %collective-permute-start.10) | collective-permute-done | bytes 53280 | tf_op jit(solution)/shard_map/ppermute | solution.py:499
  53.2 0.6 collective-permute-done.9
  53.8 0.2 collective-permute-done.8
  54.0 4.9 %collective-permute-start.11 = (f32[104,128]{1,0:T(8,128)S(1)}, f32[104,128]{1,0:T(8,128)S(1)}, u32[]{:S(2)}, u32[]{:S(2)}) collective-permute-start(f32[104,128]{1,0:T(8,128)S(1)} %add_add_fusion.own_ref), channel_id=1, source_target_pairs={{0,1},{1,0},{2,3},{3,2},{4,5},{5,4},{6,7},{7,6},{8,9},{9,8},{10,11... | collective-permute-start | bytes 159752 | tf_op jit(solution)/shard_map/ppermute | solution.py:493
  59.0 0.9 %collective-permute-done.11.other_ref = f32[104,128]{1,0:T(8,128)S(1)} collective-permute-done((f32[104,128]{1,0:T(8,128)S(1)}, f32[104,128]{1,0:T(8,128)S(1)}, u32[]{:S(2)}, u32[]{:S(2)}) %collective-permute-start.11) | collective-permute-done | bytes 53280 | tf_op jit(solution)/shard_map/ppermute | solution.py:493
  59.8 0.7 %finish.1 = (f32[64,192]{1,0:T(8,128)}, f32[64,192]{1,0:T(8,128)}, f32[2,128]{1,0:T(2,128)}) custom-call(s32[1]{0:T(128)} %bitcast.me_ref, f32[104,128]{1,0:T(8,128)S(1)} %add_add_fusion.own_ref, f32[104,128]{1,0:T(8,128)S(1)} %collective-permute-done.11.other_ref), custom_call_target="tpu_custom_call" | custom-call | tf_op jit(solution)/shard_map/finish/pallas_call | solution.py:567
  (4 shorter events, 0.1 us)
Async XLA Ops:
  23.9 3.1 %collective-permute-start = (f32[16,40,128]{2,1,0:T(8,128)S(1)}, f32[16,40,128]{2,1,0:T(8,128)S(1)}, u32[]{:S(2)}, u32[]{:S(2)}) collective-permute-start(f32[16,40,128]{2,1,0:T(8,128)S(1)} %all_to_all.5.own_ref), channel_id=1, source_target_pairs={{0,1},{1,0},{2,3},{3,2},{4,5},{5,4},{6,7},{7,6},{8,9},{9,8},{10,11... | collective-permute-start | bytes 983048 | tf_op jit(solution)/shard_map/ppermute | solution.py:493
  33.9 1.3 %collective-permute-start.1 = (f32[104,128]{1,0:T(8,128)S(1)}, f32[104,128]{1,0:T(8,128)S(1)}, u32[]{:S(2)}, u32[]{:S(2)}) collective-permute-start(f32[104,128]{1,0:T(8,128)S(1)} %get-tuple-element.33), channel_id=1, source_target_pairs={{0,1},{1,0},{2,3},{3,2},{4,5},{5,4},{6,7},{7,6},{8,9},{9,8},{10,11... | collective-permute-start | bytes 159752 | tf_op jit(solution)/shard_map/ppermute | solution.py:493
  35.2 5.6 %collective-permute-start.4 = (f32[104,128]{1,0:T(8,128)S(1)}, f32[104,128]{1,0:T(8,128)S(1)}, u32[]{:S(2)}, u32[]{:S(2)}) collective-permute-start(f32[104,128]{1,0:T(8,128)S(1)} %add.30), channel_id=1, source_target_pairs={{0,64},{32,96},{64,0},{96,32},{1,65},{33,97},{65,1},{97,33},{2,66}... | collective-permute-start | bytes 159752 | tf_op jit(solution)/shard_map/ppermute | solution.py:499
  38.9 4.2 %collective-permute-start.3 = (f32[104,128]{1,0:T(8,128)S(1)}, f32[104,128]{1,0:T(8,128)S(1)}, u32[]{:S(2)}, u32[]{:S(2)}) collective-permute-start(f32[104,128]{1,0:T(8,128)S(1)} %add.30), channel_id=1, source_target_pairs={{0,96},{32,64},{64,32},{96,0},{1,97},{33,65},{65,33},{97,1},{2,98}... | collective-permute-start | bytes 159752 | tf_op jit(solution)/shard_map/ppermute | solution.py:499
  39.3 3.8 %collective-permute-start.2 = (f32[104,128]{1,0:T(8,128)S(1)}, f32[104,128]{1,0:T(8,128)S(1)}, u32[]{:S(2)}, u32[]{:S(2)}) collective-permute-start(f32[104,128]{1,0:T(8,128)S(1)} %add.30), channel_id=1, source_target_pairs={{0,32},{32,0},{64,96},{96,64},{1,33},{33,1},{65,97},{97,65},{2,34}... | collective-permute-start | bytes 159752 | tf_op jit(solution)/shard_map/ppermute | solution.py:499
  43.1 4.6 %collective-permute-start.7 = (f32[104,128]{1,0:T(8,128)S(1)}, f32[104,128]{1,0:T(8,128)S(1)}, u32[]{:S(2)}, u32[]{:S(2)}) collective-permute-start(f32[104,128]{1,0:T(8,128)S(1)} %add_add_fusion.2), channel_id=1, source_target_pairs={{0,16},{1,17},{2,18},{3,19},{4,20},{5,21},{6,22},{7,23},{8,24},{9,... | collective-permute-start | bytes 159752 | tf_op jit(solution)/shard_map/ppermute | solution.py:499
  43.7 4.5 %collective-permute-start.6 = (f32[104,128]{1,0:T(8,128)S(1)}, f32[104,128]{1,0:T(8,128)S(1)}, u32[]{:S(2)}, u32[]{:S(2)}) collective-permute-start(f32[104,128]{1,0:T(8,128)S(1)} %add_add_fusion.2), channel_id=1, source_target_pairs={{0,24},{1,25},{2,26},{3,27},{4,28},{5,29},{6,30},{7,31},{8,16},{9,... | collective-permute-start | bytes 159752 | tf_op jit(solution)/shard_map/ppermute | solution.py:499
  45.2 3.5 %collective-permute-start.5 = (f32[104,128]{1,0:T(8,128)S(1)}, f32[104,128]{1,0:T(8,128)S(1)}, u32[]{:S(2)}, u32[]{:S(2)}) collective-permute-start(f32[104,128]{1,0:T(8,128)S(1)} %add_add_fusion.2), channel_id=1, source_target_pairs={{0,8},{1,9},{2,10},{3,11},{4,12},{5,13},{6,14},{7,15},{8,0},{9,1},... | collective-permute-start | bytes 159752 | tf_op jit(solution)/shard_map/ppermute | solution.py:499
  48.7 4.6 %collective-permute-start.10 = (f32[104,128]{1,0:T(8,128)S(1)}, f32[104,128]{1,0:T(8,128)S(1)}, u32[]{:S(2)}, u32[]{:S(2)}) collective-permute-start(f32[104,128]{1,0:T(8,128)S(1)} %add_add_fusion.1), channel_id=1, source_target_pairs={{0,4},{1,5},{2,6},{3,7},{4,0},{5,1},{6,2},{7,3},{8,12},{9,13},{10,... | collective-permute-start | bytes 159752 | tf_op jit(solution)/shard_map/ppermute | solution.py:499
  49.6 4.2 %collective-permute-start.9 = (f32[104,128]{1,0:T(8,128)S(1)}, f32[104,128]{1,0:T(8,128)S(1)}, u32[]{:S(2)}, u32[]{:S(2)}) collective-permute-start(f32[104,128]{1,0:T(8,128)S(1)} %add_add_fusion.1), channel_id=1, source_target_pairs={{0,6},{1,7},{2,4},{3,5},{4,2},{5,3},{6,0},{7,1},{8,14},{9,15},{10,... | collective-permute-start | bytes 159752 | tf_op jit(solution)/shard_map/ppermute | solution.py:499
  51.0 3.0 %collective-permute-start.8 = (f32[104,128]{1,0:T(8,128)S(1)}, f32[104,128]{1,0:T(8,128)S(1)}, u32[]{:S(2)}, u32[]{:S(2)}) collective-permute-start(f32[104,128]{1,0:T(8,128)S(1)} %add_add_fusion.1), channel_id=1, source_target_pairs={{0,2},{1,3},{2,0},{3,1},{4,6},{5,7},{6,4},{7,5},{8,10},{9,11},{10,... | collective-permute-start | bytes 159752 | tf_op jit(solution)/shard_map/ppermute | solution.py:499
  54.0 5.8 %collective-permute-start.11 = (f32[104,128]{1,0:T(8,128)S(1)}, f32[104,128]{1,0:T(8,128)S(1)}, u32[]{:S(2)}, u32[]{:S(2)}) collective-permute-start(f32[104,128]{1,0:T(8,128)S(1)} %add_add_fusion.own_ref), channel_id=1, source_target_pairs={{0,1},{1,0},{2,3},{3,2},{4,5},{5,4},{6,7},{7,6},{8,9},{9,8},{10,11... | collective-permute-start | bytes 159752 | tf_op jit(solution)/shard_map/ppermute | solution.py:493
